TPU v7x, 256 devices: a whole 4x4x8 slice. The times are simulated.
256 devices in a mesh: ctx: 16 (over x, y_hi, core), ch: 16 (over z, y_lo).
Axes of the slice: x: 4, y: 4 (y_hi: 2, y_lo: 2; y = y_hi * 2 + y_lo), z: 8, core: 2. Of those that a mesh axis runs over, the one named last changes fastest.
Arguments:
- out_gate: bfloat16 [2048, 8192], P('ctx', 'ch'), may hold values from -6 to 6
- in_gate: bfloat16 [2048, 8192], P('ctx', 'ch'), may hold values from -6 to 6
- values: bfloat16 [2048, 8192], P('ctx', 'ch'), may hold values from -6 to 6
- filter_taps: bfloat16 [2048, 8192], P(None, 'ch'), may hold values from -1.1 to 1.1, as said below
- upstream: bfloat16 [2048, 8192], P('ctx', 'ch'), may hold values from -6 to 6
Outputs:
- mixed_out: bfloat16 [2048, 8192], P('ctx', 'ch')
- grad_out_gate: bfloat16 [2048, 8192], P('ctx', 'ch')
- grad_in_gate: bfloat16 [2048, 8192], P('ctx', 'ch')
- grad_values: bfloat16 [2048, 8192], P('ctx', 'ch')
- grad_filter: float32 [2048, 8192], P(('ctx', 'ch'))
Inputs may be any that keep to these rules, and one draw needn't show every extreme that they name: `filter_taps`: taps of the causal filter, lag first.
All inputs are finite; a program needn't handle non-finite values.
Results may differ from a plain program's by a relative error of at most 0.0049.
Values may be sent and summed in bfloat16 or wider, within the bound.
No kernel may reach another device: no remote copies, remote signals or barrier semaphores. Data moves between devices by JAX's collectives and lax.ppermute only.
A program may use at most 64 MiB of HBM per device.

v0:
```python
import math

import jax
import jax.numpy as jnp
import ml_dtypes
import numpy as np
from jax import lax
from jax.experimental import pallas as pl
from jax.experimental.pallas import tpu as pltpu
from jax.sharding import PartitionSpec as P

VMEM = 48 * 1024 * 1024
f32, bf16 = jnp.float32, jnp.bfloat16


def leaf_angles(count, theta):
    if count == 1:
        return [theta]
    return leaf_angles(count // 2, theta / 2) + leaf_angles(count // 2, theta / 2 + math.pi)


def evaluate(coefs, theta):
    if len(coefs) == 1:
        return coefs
    half = len(coefs) // 2
    wr, wi = math.cos(theta / 2), math.sin(theta / 2)
    plus, minus = [], []
    for (lr, li), (hr, hi) in zip(coefs[:half], coefs[half:]):
        if hi is None:
            tr, ti = hr * wr, hr * wi
            plus.append((lr + tr, ti))
            minus.append((lr - tr, -ti))
        else:
            tr, ti = hr * wr - hi * wi, hr * wi + hi * wr
            plus.append((lr + tr, li + ti))
            minus.append((lr - tr, li - ti))
    return evaluate(plus, theta / 2) + evaluate(minus, theta / 2 + math.pi)


def interpolate(values, theta, real):
    if len(values) == 1:
        return values
    half = len(values) // 2
    wr, wi = math.cos(theta / 2), math.sin(theta / 2)
    plus = interpolate(values[:half], theta / 2, False)
    minus = interpolate(values[half:], theta / 2 + math.pi, False)
    low, high = [], []
    for (pr, pi), (mr, mi) in zip(plus, minus):
        dr, di = pr - mr, pi - mi
        if real:
            low.append(pr + mr)
            high.append(dr * wr + di * wi)
        else:
            low.append((pr + mr, pi + mi))
            high.append((dr * wr + di * wi, di * wr - dr * wi))
    return low + high


def tables(blocks, outer):
    phi = np.array(leaf_angles(blocks, math.pi / 2))
    b = np.arange(outer)
    twist = np.exp(1j * phi[:, None] * b[None, :] / outer)
    twist = np.concatenate([twist.real, twist.imag], 0).astype(np.float32)
    w = np.exp(2j * np.pi * (np.outer(b, b) % outer) / outer)
    forward = np.block([[w.real, w.imag], [-w.imag, w.real]])
    v = np.conj(w) / (blocks * outer)
    backward = np.block([[v.real, v.imag], [-v.imag, v.real]])

    def split(m):
        top = m.astype(np.float32).astype(ml_dtypes.bfloat16)
        rest = (m - top.astype(np.float64)).astype(np.float32).astype(ml_dtypes.bfloat16)
        return np.stack([top, rest])

    return twist, split(forward), split(backward)


def accurate_dot(x, m_ref):
    top = x.astype(bf16)
    rest = (x - top.astype(f32)).astype(bf16)
    dot = lambda a, b: jnp.dot(a, b, preferred_element_type=f32)
    return dot(top, m_ref[0]) + (dot(rest, m_ref[0]) + dot(top, m_ref[1]))


def send_kernel(out_gate, in_gate, values, upstream, send):
    blocks, width = send.shape[0], send.shape[1] // 2
    product = (in_gate[...].astype(f32) * values[...].astype(f32)).astype(bf16)
    cotangent = (upstream[...].astype(f32) * out_gate[...].astype(f32)).astype(bf16)
    rows = product.shape[0]
    send[:, :width, :] = product.T.reshape(blocks, width, rows)
    send[:, width:, :] = cotangent.T.reshape(blocks, width, rows)


def forward_part(load, twist, matrix, work, width, outer):
    blocks = twist.shape[0] // 2
    for g in range(width // 16):
        coefs = [(load(i, g), None) for i in range(blocks)]
        for k, (re, im) in enumerate(evaluate(coefs, math.pi / 2)):
            cr, ci = twist[k : k + 1, :], twist[blocks + k : blocks + k + 1, :]
            at = slice(k * width + 16 * g, k * width + 16 * g + 16)
            work[at, :outer] = re * cr - im * ci
            work[at, outer:] = re * ci + im * cr
    step = 128
    for r in range(0, blocks * width, step):
        work[r : r + step, :] = accurate_dot(work[r : r + step, :], matrix)


def taps_kernel(index, taps, twist, matrix, spectrum, turned):
    blocks, outer = twist.shape[0] // 2, twist.shape[1]
    width = spectrum.shape[0] // blocks
    for i in range(blocks):
        turned[i] = taps[i * outer : (i + 1) * outer, :].astype(f32).T
    start = pl.multiple_of(index[1], 16)

    def load(i, g):
        return turned[i, pl.ds(start + 16 * g, 16), :]

    forward_part(load, twist, matrix, spectrum, width, outer)


def mix_kernel(received, taps_values, twist, forward, backward, result, work):
    blocks, width, outer = received.shape[0], received.shape[1] // 2, received.shape[2]
    for s in range(2):
        forward_part(
            lambda i, g: received[i, s * width + 16 * g : s * width + 16 * g + 16, :].astype(f32),
            twist, forward, work.at[s], width, outer,
        )
    step = 128
    for r in range(0, blocks * width, step):
        at = slice(r, r + step)
        pr, pi = work[0, at, :outer], work[0, at, outer:]
        cr, ci = work[1, at, :outer], work[1, at, outer:]
        hr, hi = taps_values[at, :outer], taps_values[at, outer:]
        filtered = jnp.concatenate([hr * pr - hi * pi, hr * pi + hi * pr], 1)
        mixed = jnp.concatenate([cr * hr + ci * hi, ci * hr - cr * hi], 1)
        lags = jnp.concatenate([cr * pr + ci * pi, ci * pr - cr * pi], 1)
        work[0, at, :] = accurate_dot(filtered, backward)
        work[1, at, :] = accurate_dot(mixed, backward)
        work[2, at, :] = accurate_dot(lags, backward)
    norm_factor = (blocks * outer) ** -0.5
    for s in range(3):
        for g in range(width // 16):
            values = []
            for k in range(blocks):
                cr, ci = twist[k : k + 1, :], twist[blocks + k : blocks + k + 1, :]
                at = slice(k * width + 16 * g, k * width + 16 * g + 16)
                re, im = work[s, at, :outer], work[s, at, outer:]
                values.append((re * cr + im * ci, im * cr - re * ci))
            for i, x in enumerate(interpolate(values, math.pi / 2, True)):
                if s == 2:
                    x = x * norm_factor
                result[i, s * width + 16 * g : s * width + 16 * g + 16, :] = x.astype(bf16)


def lags_kernel(back, lags):
    width = back.shape[1] // 3
    part = back[:, 2 * width :, :].astype(f32)
    turned = part.reshape(part.shape[0] * width, part.shape[2]).T
    lags[...] = turned.reshape(lags.shape)


def gates_kernel(back, out_gate, in_gate, values, upstream, mixed_out, d_out_gate, d_in_gate, d_values):
    width = back.shape[1] // 3
    rows = back.shape[2]

    def part(s):
        x = back[:, s * width : (s + 1) * width, :].astype(f32)
        return x.reshape(x.shape[0] * width, rows).T

    filtered, grad_mixed = part(0), part(1)
    mixed_out[...] = (out_gate[...].astype(f32) * filtered).astype(bf16)
    d_out_gate[...] = (upstream[...].astype(f32) * filtered).astype(bf16)
    d_in_gate[...] = (grad_mixed * values[...].astype(f32)).astype(bf16)
    d_values[...] = (grad_mixed * in_gate[...].astype(f32)).astype(bf16)


def join_kernel(arrived, grad_filter):
    span = arrived.shape[2]
    for j in range(arrived.shape[0]):
        grad_filter[:, j * span : (j + 1) * span] = arrived[j].astype(f32)


def call(kernel, outs, *args, flops=1000000, **kwargs):
    return pl.pallas_call(
        kernel,
        out_shape=outs,
        compiler_params=pltpu.CompilerParams(vmem_limit_bytes=VMEM),
        cost_estimate=pl.CostEstimate(flops=flops, bytes_accessed=1 << 20, transcendentals=0),
        **kwargs,
    )(*args)


def body(out_gate, in_gate, values, filter_taps, upstream):
    rows, channels = out_gate.shape
    seq_len = filter_taps.shape[0]
    blocks = lax.axis_size("ctx")
    owners = lax.axis_size("ch")
    width = channels // blocks
    shape = jax.ShapeDtypeStruct
    twist, forward, backward = (jnp.asarray(t) for t in tables(blocks, rows))

    send = call(send_kernel, shape((blocks, 2 * width, rows), bf16), out_gate, in_gate, values, upstream)
    received = lax.all_to_all(send, "ctx", 0, 0, tiled=True)

    me = lax.axis_index("ctx")
    first = me * width
    index = jnp.stack([first // 128, first % 128]).astype(jnp.int32)
    whole = lambda s: pl.BlockSpec(s, lambda g, index: (0,) * len(s))
    taps_values = call(
        taps_kernel,
        shape((blocks * width, 2 * rows), f32),
        index, filter_taps, twist, forward,
        grid_spec=pltpu.PrefetchScalarGridSpec(
            num_scalar_prefetch=1,
            grid=(1,),
            in_specs=[
                pl.BlockSpec((seq_len, 128), lambda g, index: (0, index[0])),
                whole(twist.shape),
                whole(forward.shape),
            ],
            out_specs=whole((blocks * width, 2 * rows)),
            scratch_shapes=[pltpu.VMEM((blocks, 128, rows), f32)],
        ),
    )
    result = call(
        mix_kernel,
        shape((blocks, 3 * width, rows), bf16),
        received, taps_values, twist, forward, backward,
        scratch_shapes=[pltpu.VMEM((3, blocks * width, 2 * rows), f32)],
    )
    back = lax.all_to_all(result, "ctx", 0, 0, tiled=True)
    lags = call(lags_kernel, shape((owners, rows // owners, channels), f32), back)
    arrived = lax.all_to_all(lags, "ch", 0, 0, tiled=True)
    out = shape((rows, channels), bf16)
    gates = call(gates_kernel, (out,) * 4, back, out_gate, in_gate, values, upstream)
    grad_filter = call(join_kernel, shape((rows // owners, owners * channels), f32), arrived)
    return (*gates, grad_filter)


def solution(mesh):
    return jax.shard_map(
        body,
        mesh=mesh,
        in_specs=(P("ctx", "ch"), P("ctx", "ch"), P("ctx", "ch"), P(None, "ch"), P("ctx", "ch")),
        out_specs=(
            P("ctx", "ch"),
            P("ctx", "ch"),
            P("ctx", "ch"),
            P("ctx", "ch"),
            P(("ctx", "ch"), None),
        ),
        check_vma=False,
    )
```

profile of v0, /device:TPU:1, one launch (start us, length us, event | category | flops | bytes accessed | tf_op | source)
XLA Modules:
  0.0 57.4 jit_solution(17865542940972100513)
XLA Ops:
  0.6 0.0 copy-start.2
  0.6 0.0 copy-start.3
  0.7 0.9 %copy-done.3 = bf16[128,512]{1,0:T(8,128)(2,1)S(1)} copy-done((bf16[128,512]{1,0:T(8,128)(2,1)S(1)}, bf16[128,512]{1,0:T(8,128)(2,1)}, u32[]{:S(2)}) %copy-start.3) | copy-done | bytes 131096
  1.6 0.9 %copy-done.5 = bf16[128,512]{1,0:T(8,128)(2,1)S(1)} copy-done((bf16[128,512]{1,0:T(8,128)(2,1)S(1)}, bf16[128,512]{1,0:T(8,128)(2,1)}, u32[]{:S(2)}) %copy-start.5) | copy-done | bytes 131096
  2.5 0.9 %copy-done.7 = bf16[128,512]{1,0:T(8,128)(2,1)S(1)} copy-done((bf16[128,512]{1,0:T(8,128)(2,1)S(1)}, bf16[128,512]{1,0:T(8,128)(2,1)}, u32[]{:S(2)}) %copy-start.7) | copy-done | bytes 131096
  3.4 0.9 %copy-done.9 = bf16[128,512]{1,0:T(8,128)(2,1)S(1)} copy-done((bf16[128,512]{1,0:T(8,128)(2,1)S(1)}, bf16[128,512]{1,0:T(8,128)(2,1)}, u32[]{:S(2)}) %copy-start.9) | copy-done | bytes 131096
  4.3 0.8 %shard_map.119 = bf16[16,64,128]{2,1,0:T(8,128)(2,1)} custom-call(bf16[128,512]{1,0:T(8,128)(2,1)S(1)} %copy-done.3, bf16[128,512]{1,0:T(8,128)(2,1)S(1)} %copy-done.5, bf16[128,512]{1,0:T(8,128)(2,1)S(1)} %copy-done.7, bf16[128,512]{1,0:T(8,128)(2,1)S(1)} %copy-done.9), custom_call_target="tpu_custom_call" | custom-call | flops 1000000 | bytes 1048576 | tf_op jit(solution)/shard_map/pallas_call | solution.py:183
  5.1 8.4 %all-to-all-start = ((bf16[16,64,128]{2,1,0:T(8,128)(2,1)}), bf16[16,64,128]{2,1,0:T(8,128)(2,1)S(1)}, u32[]{:S(2)}, u32[]{:S(2)}) async-start(bf16[16,64,128]{2,1,0:T(8,128)(2,1)} %shard_map.119), calls=%async_computation | async-start | bytes 524288 | tf_op jit(solution)/shard_map/all_to_all | solution.py:202
  13.6 0.1 pad_add_fusion.index
  13.7 1.6 %copy-done = bf16[2048,512]{1,0:T(8,128)(2,1)S(1)} copy-done((bf16[2048,512]{1,0:T(8,128)(2,1)S(1)}, bf16[2048,512]{1,0:T(8,128)(2,1)}, u32[]{:S(2)}) %copy-start) | copy-done | bytes 2097176
  15.3 0.9 %copy-done.1 = bf16[2,256,256]{2,1,0:T(8,128)(2,1)S(1)} copy-done((bf16[2,256,256]{2,1,0:T(8,128)(2,1)S(1)}, bf16[2,256,256]{2,1,0:T(8,128)(2,1)}, u32[]{:S(2)}) %copy-start.1) | copy-done | bytes 262168
  16.2 0.7 %copy-done.12 = f32[32,128]{1,0:T(8,128)S(1)} copy-done((f32[32,128]{1,0:T(8,128)S(1)}, f32[32,128]{1,0:T(8,128)}, u32[]{:S(2)}) %copy-start.12) | copy-done | bytes 16408
  16.9 1.3 %shard_map.120.taps_values = f32[512,256]{1,0:T(8,128)S(1)} custom-call(s32[2]{0:T(128)S(1)} %pad_add_fusion.index, bf16[2048,512]{1,0:T(8,128)(2,1)S(1)} %copy-done, f32[32,128]{1,0:T(8,128)S(1)} %copy-done.12, bf16[2,256,256]{2,1,0:T(8,128)(2,1)S(1)} %copy-done.1), custom_call_target="tpu_custom_call" | custom-call | flops 1000000 | bytes 1048576 | tf_op jit(solution)/shard_map/pallas_call | solution.py:183
  18.2 0.0 copy-start.4
  18.2 0.0 copy-start.6
  18.2 0.0 copy-start.10
  18.2 4.2 %all-to-all-done.received = bf16[16,64,128]{2,1,0:T(8,128)(2,1)S(1)} async-done(((bf16[16,64,128]{2,1,0:T(8,128)(2,1)}), bf16[16,64,128]{2,1,0:T(8,128)(2,1)S(1)}, u32[]{:S(2)}, u32[]{:S(2)}) %all-to-all-start) | async-done | bytes 262176 | tf_op jit(solution)/shard_map/all_to_all | solution.py:202
  22.5 1.8 %shard_map.121 = bf16[16,96,128]{2,1,0:T(8,128)(2,1)S(1)} custom-call(bf16[16,64,128]{2,1,0:T(8,128)(2,1)S(1)} %all-to-all-done.received, f32[512,256]{1,0:T(8,128)S(1)} %shard_map.120.taps_values, f32[32,128]{1,0:T(8,128)S(1)} %copy-done.13, bf16[2,256,256]{2,1,0:T(8,128)(2,1)S(1)} %copy-done.2, bf16[2,256,256]{2,1,0:T(8,128)(2,1)S(1)} %copy-done.11), custom_call_target="tpu_custom_call" | custom-call | flops 1000000 | bytes 1048576 | tf_op jit(solution)/shard_map/pallas_call | solution.py:183
  24.3 13.0 %all_to_all.15.back = bf16[16,96,128]{2,1,0:T(8,128)(2,1)S(1)} all-to-all(bf16[16,96,128]{2,1,0:T(8,128)(2,1)S(1)} %shard_map.121), channel_id=1, replica_groups=mesh['ctx'=16,'ch'=16] {'ctx'}, dimensions={0} | all-to-all | bytes 786432 | tf_op jit(solution)/shard_map/all_to_all | solution.py:230
  37.3 0.8 %shard_map.123 = f32[16,8,512]{2,1,0:T(8,128)} custom-call(bf16[16,96,128]{2,1,0:T(8,128)(2,1)S(1)} %all_to_all.15.back), custom_call_target="tpu_custom_call" | custom-call | flops 1000000 | bytes 1048576 | tf_op jit(solution)/shard_map/pallas_call | solution.py:183
  38.1 8.4 %all-to-all-start.2 = ((f32[16,8,512]{2,1,0:T(8,128)}), f32[16,8,512]{2,1,0:T(8,128)S(1)}, u32[]{:S(2)}, u32[]{:S(2)}) async-start(f32[16,8,512]{2,1,0:T(8,128)} %shard_map.123), calls=%async_computation.2 | async-start | bytes 524288 | tf_op jit(solution)/shard_map/all_to_all | solution.py:232
  46.5 0.9 %shard_map.122 = (bf16[128,512]{1,0:T(8,128)(2,1)}, bf16[128,512]{1,0:T(8,128)(2,1)}, bf16[128,512]{1,0:T(8,128)(2,1)}, bf16[128,512]{1,0:T(8,128)(2,1)}) custom-call(bf16[16,96,128]{2,1,0:T(8,128)(2,1)S(1)} %all_to_all.15.back, bf16[128,512]{1,0:T(8,128)(2,1)S(1)} %copy-done.4, bf16[128,512]{1,0:T(8,128)(2,1)S(1)} %copy-done.6, ...), custom_call_target="tpu_custom_call" | custom-call | flops 1000000 | bytes 1048576 | tf_op jit(solution)/shard_map/pallas_call | solution.py:183
  47.4 9.2 %all-to-all-done.2.arrived = f32[16,8,512]{2,1,0:T(8,128)S(1)} async-done(((f32[16,8,512]{2,1,0:T(8,128)}), f32[16,8,512]{2,1,0:T(8,128)S(1)}, u32[]{:S(2)}, u32[]{:S(2)}) %all-to-all-start.2) | async-done | bytes 262176 | tf_op jit(solution)/shard_map/all_to_all | solution.py:232
  56.6 0.7 %shard_map.124 = f32[8,8192]{1,0:T(8,128)} custom-call(f32[16,8,512]{2,1,0:T(8,128)S(1)} %all-to-all-done.2.arrived), custom_call_target="tpu_custom_call" | custom-call | flops 1000000 | bytes 1048576 | tf_op jit(solution)/shard_map/pallas_call | solution.py:183
  (16 shorter events, 0.0 us)
Async XLA Ops:
  0.6 21.9 %copy-start.2 = (bf16[2,256,256]{2,1,0:T(8,128)(2,1)S(1)}, bf16[2,256,256]{2,1,0:T(8,128)(2,1)}, u32[]{:S(2)}) copy-start(bf16[2,256,256]{2,1,0:T(8,128)(2,1)} %constant.40.clone.matrix.forward) | copy-start | bytes 786436
  0.6 0.9 %copy-start.3 = (bf16[128,512]{1,0:T(8,128)(2,1)S(1)}, bf16[128,512]{1,0:T(8,128)(2,1)}, u32[]{:S(2)}) copy-start(bf16[128,512]{1,0:T(8,128)(2,1)} %out_gate.3) | copy-start | bytes 393220
  1.6 0.9 %copy-start.5 = (bf16[128,512]{1,0:T(8,128)(2,1)S(1)}, bf16[128,512]{1,0:T(8,128)(2,1)}, u32[]{:S(2)}) copy-start(bf16[128,512]{1,0:T(8,128)(2,1)} %in_gate.3) | copy-start | bytes 393220
  2.5 0.9 %copy-start.7 = (bf16[128,512]{1,0:T(8,128)(2,1)S(1)}, bf16[128,512]{1,0:T(8,128)(2,1)}, u32[]{:S(2)}) copy-start(bf16[128,512]{1,0:T(8,128)(2,1)} %values.3) | copy-start | bytes 393220
  3.4 0.9 %copy-start.9 = (bf16[128,512]{1,0:T(8,128)(2,1)S(1)}, bf16[128,512]{1,0:T(8,128)(2,1)}, u32[]{:S(2)}) copy-start(bf16[128,512]{1,0:T(8,128)(2,1)} %upstream.3) | copy-start | bytes 393220
  4.3 18.2 %copy-start.11 = (bf16[2,256,256]{2,1,0:T(8,128)(2,1)S(1)}, bf16[2,256,256]{2,1,0:T(8,128)(2,1)}, u32[]{:S(2)}) copy-start(bf16[2,256,256]{2,1,0:T(8,128)(2,1)} %constant.41.clone.backward) | copy-start | bytes 786436
  4.3 18.2 %copy-start.13 = (f32[32,128]{1,0:T(8,128)S(1)}, f32[32,128]{1,0:T(8,128)}, u32[]{:S(2)}) copy-start(f32[32,128]{1,0:T(8,128)} %constant.39.clone.twist) | copy-start | bytes 49156
  5.1 17.4 %all-to-all-start = ((bf16[16,64,128]{2,1,0:T(8,128)(2,1)}), bf16[16,64,128]{2,1,0:T(8,128)(2,1)S(1)}, u32[]{:S(2)}, u32[]{:S(2)}) async-start(bf16[16,64,128]{2,1,0:T(8,128)(2,1)} %shard_map.119), calls=%async_computation | async-start | bytes 524288 | tf_op jit(solution)/shard_map/all_to_all | solution.py:202
  13.7 1.6 %copy-start = (bf16[2048,512]{1,0:T(8,128)(2,1)S(1)}, bf16[2048,512]{1,0:T(8,128)(2,1)}, u32[]{:S(2)}) copy-start(bf16[2048,512]{1,0:T(8,128)(2,1)} %taps.1) | copy-start | bytes 6291460
  15.3 0.9 %copy-start.1 = (bf16[2,256,256]{2,1,0:T(8,128)(2,1)S(1)}, bf16[2,256,256]{2,1,0:T(8,128)(2,1)}, u32[]{:S(2)}) copy-start(bf16[2,256,256]{2,1,0:T(8,128)(2,1)} %constant.40.clone.matrix.forward) | copy-start | bytes 786436
  16.2 0.7 %copy-start.12 = (f32[32,128]{1,0:T(8,128)S(1)}, f32[32,128]{1,0:T(8,128)}, u32[]{:S(2)}) copy-start(f32[32,128]{1,0:T(8,128)} %constant.39.clone.twist) | copy-start | bytes 49156
  18.2 28.3 %copy-start.4 = (bf16[128,512]{1,0:T(8,128)(2,1)S(1)}, bf16[128,512]{1,0:T(8,128)(2,1)}, u32[]{:S(2)}) copy-start(bf16[128,512]{1,0:T(8,128)(2,1)} %out_gate.3) | copy-start | bytes 393220
  18.2 28.3 %copy-start.6 = (bf16[128,512]{1,0:T(8,128)(2,1)S(1)}, bf16[128,512]{1,0:T(8,128)(2,1)}, u32[]{:S(2)}) copy-start(bf16[128,512]{1,0:T(8,128)(2,1)} %in_gate.3) | copy-start | bytes 393220
  18.2 28.3 %copy-start.8 = (bf16[128,512]{1,0:T(8,128)(2,1)S(1)}, bf16[128,512]{1,0:T(8,128)(2,1)}, u32[]{:S(2)}) copy-start(bf16[128,512]{1,0:T(8,128)(2,1)} %values.3) | copy-start | bytes 393220
  18.2 28.3 %copy-start.10 = (bf16[128,512]{1,0:T(8,128)(2,1)S(1)}, bf16[128,512]{1,0:T(8,128)(2,1)}, u32[]{:S(2)}) copy-start(bf16[128,512]{1,0:T(8,128)(2,1)} %upstream.3) | copy-start | bytes 393220
  38.1 18.6 %all-to-all-start.2 = ((f32[16,8,512]{2,1,0:T(8,128)}), f32[16,8,512]{2,1,0:T(8,128)S(1)}, u32[]{:S(2)}, u32[]{:S(2)}) async-start(f32[16,8,512]{2,1,0:T(8,128)} %shard_map.123), calls=%async_computation.2 | async-start | bytes 524288 | tf_op jit(solution)/shard_map/all_to_all | solution.py:232
where the time goes:
time: 58.1 us; the launch traced here: 57.4 us
  starting transfers between devices  16.9 us (29%)
  waiting for transfers between devices  13.4 us (23%)
  blocking collectives  13 us (22%)
  local copies, waits for them, and re-layouts  6.95 us (12%)
  Pallas kernels  6.34 us (11%)
  between operations  0.75 us (1%)
    all_to_all x1, blocking collectives, body(): back = lax.all_to_all(result, 'ctx', 0, 0, tiled=True)  13 us
    all_to_all x1, waiting for transfers between devices, body(): arrived = lax.all_to_all(lags, 'ch', 0, 0, tiled=True)  9.2 us
    all_to_all x1, starting transfers between devices, body(): received = lax.all_to_all(send, 'ctx', 0, 0, tiled=True)  8.45 us
    all_to_all x1, starting transfers between devices, body(): arrived = lax.all_to_all(lags, 'ch', 0, 0, tiled=True)  8.4 us
    unnamed x28, local copies, waits for them, and re-layouts  6.95 us
    pallas_call x6, Pallas kernels, call(): pl.pallas_call(kernel, out_shape=outs, compiler_params=pltpu.CompilerPara...  6.34 us
    all_to_all x1, waiting for transfers between devices, body(): received = lax.all_to_all(send, 'ctx', 0, 0, tiled=True)  4.24 us
  transfers between devices with their start and end apart: 2, of which 2 were waited for; matrix products, arithmetic and copies ran while one was open for 0% of the time, Pallas kernels for 4%

commit v1 on v0

--- a/solution.py
+++ b/solution.py
@@ -10,6 +10,7 @@
 from jax.sharding import PartitionSpec as P
 
 VMEM = 48 * 1024 * 1024
+PARTS = 2
 f32, bf16 = jnp.float32, jnp.bfloat16
 
 
@@ -81,13 +82,28 @@
     return dot(top, m_ref[0]) + (dot(rest, m_ref[0]) + dot(top, m_ref[1]))
 
 
-def send_kernel(out_gate, in_gate, values, upstream, send):
+def send_kernel(out_gate, in_gate, values, upstream, send, held, arrived):
     blocks, width = send.shape[0], send.shape[1] // 2
-    product = (in_gate[...].astype(f32) * values[...].astype(f32)).astype(bf16)
-    cotangent = (upstream[...].astype(f32) * out_gate[...].astype(f32)).astype(bf16)
-    rows = product.shape[0]
-    send[:, :width, :] = product.T.reshape(blocks, width, rows)
-    send[:, width:, :] = cotangent.T.reshape(blocks, width, rows)
+    rows, channels = out_gate.shape
+    part = channels // PARTS
+    sources = (in_gate, values, upstream, out_gate)
+
+    def fetch(n, p):
+        at = slice(p * part, (p + 1) * part)
+        return pltpu.make_async_copy(sources[n].at[:, at], held.at[n, p], arrived.at[n, p])
+
+    for p in range(PARTS):
+        for n in range(4):
+            fetch(n, p).start()
+    for p in range(PARTS):
+        first = p * part // width
+        for s in range(2):
+            fetch(2 * s, p).wait()
+            fetch(2 * s + 1, p).wait()
+            gated = (held[2 * s, p].astype(f32) * held[2 * s + 1, p].astype(f32)).astype(bf16)
+            send[first : first + part // width, s * width : (s + 1) * width, :] = gated.T.reshape(
+                part // width, width, rows
+            )
 
 
 def forward_part(load, twist, matrix, work, width, outer):
@@ -155,7 +171,7 @@
     width = back.shape[1] // 3
     part = back[:, 2 * width :, :].astype(f32)
     turned = part.reshape(part.shape[0] * width, part.shape[2]).T
-    lags[...] = turned.reshape(lags.shape)
+    lags[...] = turned.reshape(lags.shape).astype(bf16)
 
 
 def gates_kernel(back, out_gate, in_gate, values, upstream, mixed_out, d_out_gate, d_in_gate, d_values):
@@ -179,11 +195,11 @@
         grad_filter[:, j * span : (j + 1) * span] = arrived[j].astype(f32)
 
 
-def call(kernel, outs, *args, flops=1000000, **kwargs):
+def call(kernel, outs, *args, flops=1000000, vmem=VMEM, **kwargs):
     return pl.pallas_call(
         kernel,
         out_shape=outs,
-        compiler_params=pltpu.CompilerParams(vmem_limit_bytes=VMEM),
+        compiler_params=pltpu.CompilerParams(vmem_limit_bytes=vmem),
         cost_estimate=pl.CostEstimate(flops=flops, bytes_accessed=1 << 20, transcendentals=0),
         **kwargs,
     )(*args)
@@ -198,7 +214,17 @@
     shape = jax.ShapeDtypeStruct
     twist, forward, backward = (jnp.asarray(t) for t in tables(blocks, rows))
 
-    send = call(send_kernel, shape((blocks, 2 * width, rows), bf16), out_gate, in_gate, values, upstream)
+    send = call(
+        send_kernel,
+        shape((blocks, 2 * width, rows), bf16),
+        out_gate, in_gate, values, upstream,
+        vmem=63 * 1024 * 1024 + 960 * 1024,
+        in_specs=[pl.BlockSpec(memory_space=pltpu.HBM)] * 4,
+        scratch_shapes=[
+            pltpu.VMEM((4, PARTS, rows, channels // PARTS), bf16),
+            pltpu.SemaphoreType.DMA((4, PARTS)),
+        ],
+    )
     received = lax.all_to_all(send, "ctx", 0, 0, tiled=True)
 
     me = lax.axis_index("ctx")
@@ -228,7 +254,7 @@
         scratch_shapes=[pltpu.VMEM((3, blocks * width, 2 * rows), f32)],
     )
     back = lax.all_to_all(result, "ctx", 0, 0, tiled=True)
-    lags = call(lags_kernel, shape((owners, rows // owners, channels), f32), back)
+    lags = call(lags_kernel, shape((owners, rows // owners, channels), bf16), back)
     arrived = lax.all_to_all(lags, "ch", 0, 0, tiled=True)
     out = shape((rows, channels), bf16)
     gates = call(gates_kernel, (out,) * 4, back, out_gate, in_gate, values, upstream)

time: 58.1 us -> 53.8 us (0.926)
  local copies, waits for them, and re-layouts: 6.95 us -> 3.3 us
  waiting for transfers between devices: 13.4 us -> 11.8 us
  Pallas kernels: 6.34 us -> 7.42 us
    unnamed x28 -> x20, local copies, waits for them, and re-layouts: 6.95 us -> 3.3 us
    all_to_all x1, waiting for transfers between devices: 9.2 us -> 7.53 us  [body(): arrived = lax.all_to_all(lags, 'ch', 0, 0, tiled=True)]
    pallas_call x6, Pallas kernels: 6.34 us -> 7.42 us  [call(): pl.pallas_call(kernel, out_shape=outs, compiler_params=pltpu.CompilerPara...]
where the time goes in v1:
time: 53.8 us; the launch traced here: 53.3 us
  starting transfers between devices  17 us (32%)
  blocking collectives  13 us (24%)
  waiting for transfers between devices  11.8 us (22%)
  Pallas kernels  7.42 us (14%)
  local copies, waits for them, and re-layouts  3.3 us (6%)
  between operations  0.76 us (1%)
    all_to_all x1, blocking collectives, body(): back = lax.all_to_all(result, 'ctx', 0, 0, tiled=True)  13 us
    all_to_all x1, starting transfers between devices, body(): received = lax.all_to_all(send, 'ctx', 0, 0, tiled=True)  8.59 us
    all_to_all x1, starting transfers between devices, body(): arrived = lax.all_to_all(lags, 'ch', 0, 0, tiled=True)  8.4 us
    all_to_all x1, waiting for transfers between devices, body(): arrived = lax.all_to_all(lags, 'ch', 0, 0, tiled=True)  7.53 us
    pallas_call x6, Pallas kernels, call(): pl.pallas_call(kernel, out_shape=outs, compiler_params=pltpu.CompilerPara...  7.42 us
    all_to_all x1, waiting for transfers between devices, body(): received = lax.all_to_all(send, 'ctx', 0, 0, tiled=True)  4.24 us
    unnamed x20, local copies, waits for them, and re-layouts  3.3 us
  transfers between devices with their start and end apart: 2, of which 2 were waited for; matrix products, arithmetic and copies ran while one was open for 0% of the time, Pallas kernels for 4%

profile of v1, /device:TPU:1, one launch (start us, length us, event | category | flops | bytes accessed | tf_op | source)
XLA Modules:
  0.0 53.3 jit_solution(18120273779326685374)
XLA Ops:
  0.6 2.0 %shard_map.119 = bf16[16,64,128]{2,1,0:T(8,128)(2,1)} custom-call(bf16[128,512]{1,0:T(8,128)(2,1)} %out_gate.3, bf16[128,512]{1,0:T(8,128)(2,1)} %in_gate.3, bf16[128,512]{1,0:T(8,128)(2,1)} %values.3, bf16[128,512]{1,0:T(8,128)(2,1)} %upstream.3), custom_call_target="tpu_custom_call" | custom-call | flops 1000000 | bytes 1048576 | tf_op jit(solution)/shard_map/pallas_call | solution.py:199
  2.6 0.0 copy-start.2
  2.6 0.0 copy-start.7
  2.6 0.0 copy-start.9
  2.6 8.6 %all-to-all-start = ((bf16[16,64,128]{2,1,0:T(8,128)(2,1)}), bf16[16,64,128]{2,1,0:T(8,128)(2,1)S(1)}, u32[]{:S(2)}, u32[]{:S(2)}) async-start(bf16[16,64,128]{2,1,0:T(8,128)(2,1)} %shard_map.119), calls=%async_computation | async-start | bytes 524288 | tf_op jit(solution)/shard_map/all_to_all | solution.py:228
  11.2 0.1 pad_add_fusion.index
  11.3 1.6 %copy-done = bf16[2048,512]{1,0:T(8,128)(2,1)S(1)} copy-done((bf16[2048,512]{1,0:T(8,128)(2,1)S(1)}, bf16[2048,512]{1,0:T(8,128)(2,1)}, u32[]{:S(2)}) %copy-start) | copy-done | bytes 2097176
  12.9 0.9 %copy-done.1 = bf16[2,256,256]{2,1,0:T(8,128)(2,1)S(1)} copy-done((bf16[2,256,256]{2,1,0:T(8,128)(2,1)S(1)}, bf16[2,256,256]{2,1,0:T(8,128)(2,1)}, u32[]{:S(2)}) %copy-start.1) | copy-done | bytes 262168
  13.8 0.7 %copy-done.8 = f32[32,128]{1,0:T(8,128)S(1)} copy-done((f32[32,128]{1,0:T(8,128)S(1)}, f32[32,128]{1,0:T(8,128)}, u32[]{:S(2)}) %copy-start.8) | copy-done | bytes 16408
  14.6 1.3 %shard_map.120.taps_values = f32[512,256]{1,0:T(8,128)S(1)} custom-call(s32[2]{0:T(128)S(1)} %pad_add_fusion.index, bf16[2048,512]{1,0:T(8,128)(2,1)S(1)} %copy-done, f32[32,128]{1,0:T(8,128)S(1)} %copy-done.8, bf16[2,256,256]{2,1,0:T(8,128)(2,1)S(1)} %copy-done.1), custom_call_target="tpu_custom_call" | custom-call | flops 1000000 | bytes 1048576 | tf_op jit(solution)/shard_map/pallas_call | solution.py:199
  15.8 0.0 copy-start.3
  15.8 0.0 copy-start.4
  15.9 0.0 copy-start.5
  15.9 0.0 copy-start.6
  15.9 4.2 %all-to-all-done.received = bf16[16,64,128]{2,1,0:T(8,128)(2,1)S(1)} async-done(((bf16[16,64,128]{2,1,0:T(8,128)(2,1)}), bf16[16,64,128]{2,1,0:T(8,128)(2,1)S(1)}, u32[]{:S(2)}, u32[]{:S(2)}) %all-to-all-start) | async-done | bytes 262176 | tf_op jit(solution)/shard_map/all_to_all | solution.py:228
  20.1 0.0 copy-done.2
  20.1 0.0 copy-done.7
  20.1 1.8 %shard_map.121 = bf16[16,96,128]{2,1,0:T(8,128)(2,1)S(1)} custom-call(bf16[16,64,128]{2,1,0:T(8,128)(2,1)S(1)} %all-to-all-done.received, f32[512,256]{1,0:T(8,128)S(1)} %shard_map.120.taps_values, f32[32,128]{1,0:T(8,128)S(1)} %copy-done.9, bf16[2,256,256]{2,1,0:T(8,128)(2,1)S(1)} %copy-done.2, bf16[2,256,256]{2,1,0:T(8,128)(2,1)S(1)} %copy-done.7), custom_call_target="tpu_custom_call" | custom-call | flops 1000000 | bytes 1048576 | tf_op jit(solution)/shard_map/pallas_call | solution.py:199
  21.9 13.0 %all_to_all.15.back = bf16[16,96,128]{2,1,0:T(8,128)(2,1)S(1)} all-to-all(bf16[16,96,128]{2,1,0:T(8,128)(2,1)S(1)} %shard_map.121), channel_id=1, replica_groups=mesh['ctx'=16,'ch'=16] {'ctx'}, dimensions={0} | all-to-all | bytes 786432 | tf_op jit(solution)/shard_map/all_to_all | solution.py:256
  34.9 0.8 %shard_map.123 = bf16[16,8,512]{2,1,0:T(8,128)(2,1)} custom-call(bf16[16,96,128]{2,1,0:T(8,128)(2,1)S(1)} %all_to_all.15.back), custom_call_target="tpu_custom_call" | custom-call | flops 1000000 | bytes 1048576 | tf_op jit(solution)/shard_map/pallas_call | solution.py:199
  35.7 8.4 %all-to-all-start.2 = ((bf16[16,8,512]{2,1,0:T(8,128)(2,1)}), bf16[16,8,512]{2,1,0:T(8,128)(2,1)S(1)}, u32[]{:S(2)}, u32[]{:S(2)}) async-start(bf16[16,8,512]{2,1,0:T(8,128)(2,1)} %shard_map.123), calls=%async_computation.2 | async-start | bytes 262144 | tf_op jit(solution)/shard_map/all_to_all | solution.py:258
  44.1 0.9 %shard_map.122 = (bf16[128,512]{1,0:T(8,128)(2,1)}, bf16[128,512]{1,0:T(8,128)(2,1)}, bf16[128,512]{1,0:T(8,128)(2,1)}, bf16[128,512]{1,0:T(8,128)(2,1)}) custom-call(bf16[16,96,128]{2,1,0:T(8,128)(2,1)S(1)} %all_to_all.15.back, bf16[128,512]{1,0:T(8,128)(2,1)S(1)} %copy-done.3, bf16[128,512]{1,0:T(8,128)(2,1)S(1)} %copy-done.4, ...), custom_call_target="tpu_custom_call" | custom-call | flops 1000000 | bytes 1048576 | tf_op jit(solution)/shard_map/pallas_call | solution.py:199
  45.0 7.5 %all-to-all-done.2.arrived = bf16[16,8,512]{2,1,0:T(8,128)(2,1)S(1)} async-done(((bf16[16,8,512]{2,1,0:T(8,128)(2,1)}), bf16[16,8,512]{2,1,0:T(8,128)(2,1)S(1)}, u32[]{:S(2)}, u32[]{:S(2)}) %all-to-all-start.2) | async-done | bytes 131104 | tf_op jit(solution)/shard_map/all_to_all | solution.py:258
  52.6 0.7 %shard_map.124 = f32[8,8192]{1,0:T(8,128)} custom-call(bf16[16,8,512]{2,1,0:T(8,128)(2,1)S(1)} %all-to-all-done.2.arrived), custom_call_target="tpu_custom_call" | custom-call | flops 1000000 | bytes 1048576 | tf_op jit(solution)/shard_map/pallas_call | solution.py:199
  (8 shorter events, 0.0 us)
Async XLA Ops:
  2.6 17.5 %copy-start.2 = (bf16[2,256,256]{2,1,0:T(8,128)(2,1)S(1)}, bf16[2,256,256]{2,1,0:T(8,128)(2,1)}, u32[]{:S(2)}) copy-start(bf16[2,256,256]{2,1,0:T(8,128)(2,1)} %constant.40.clone.matrix.forward) | copy-start | bytes 786436
  2.6 17.5 %copy-start.7 = (bf16[2,256,256]{2,1,0:T(8,128)(2,1)S(1)}, bf16[2,256,256]{2,1,0:T(8,128)(2,1)}, u32[]{:S(2)}) copy-start(bf16[2,256,256]{2,1,0:T(8,128)(2,1)} %constant.41.clone.backward) | copy-start | bytes 786436
  2.6 17.5 %copy-start.9 = (f32[32,128]{1,0:T(8,128)S(1)}, f32[32,128]{1,0:T(8,128)}, u32[]{:S(2)}) copy-start(f32[32,128]{1,0:T(8,128)} %constant.39.clone.twist) | copy-start | bytes 49156
  2.6 17.5 %all-to-all-start = ((bf16[16,64,128]{2,1,0:T(8,128)(2,1)}), bf16[16,64,128]{2,1,0:T(8,128)(2,1)S(1)}, u32[]{:S(2)}, u32[]{:S(2)}) async-start(bf16[16,64,128]{2,1,0:T(8,128)(2,1)} %shard_map.119), calls=%async_computation | async-start | bytes 524288 | tf_op jit(solution)/shard_map/all_to_all | solution.py:228
  11.3 1.6 %copy-start = (bf16[2048,512]{1,0:T(8,128)(2,1)S(1)}, bf16[2048,512]{1,0:T(8,128)(2,1)}, u32[]{:S(2)}) copy-start(bf16[2048,512]{1,0:T(8,128)(2,1)} %taps.1) | copy-start | bytes 6291460
  12.9 0.9 %copy-start.1 = (bf16[2,256,256]{2,1,0:T(8,128)(2,1)S(1)}, bf16[2,256,256]{2,1,0:T(8,128)(2,1)}, u32[]{:S(2)}) copy-start(bf16[2,256,256]{2,1,0:T(8,128)(2,1)} %constant.40.clone.matrix.forward) | copy-start | bytes 786436
  13.8 0.7 %copy-start.8 = (f32[32,128]{1,0:T(8,128)S(1)}, f32[32,128]{1,0:T(8,128)}, u32[]{:S(2)}) copy-start(f32[32,128]{1,0:T(8,128)} %constant.39.clone.twist) | copy-start | bytes 49156
  15.8 28.3 %copy-start.3 = (bf16[128,512]{1,0:T(8,128)(2,1)S(1)}, bf16[128,512]{1,0:T(8,128)(2,1)}, u32[]{:S(2)}) copy-start(bf16[128,512]{1,0:T(8,128)(2,1)} %out_gate.3) | copy-start | bytes 393220
  15.8 28.3 %copy-start.4 = (bf16[128,512]{1,0:T(8,128)(2,1)S(1)}, bf16[128,512]{1,0:T(8,128)(2,1)}, u32[]{:S(2)}) copy-start(bf16[128,512]{1,0:T(8,128)(2,1)} %in_gate.3) | copy-start | bytes 393220
  15.9 28.3 %copy-start.5 = (bf16[128,512]{1,0:T(8,128)(2,1)S(1)}, bf16[128,512]{1,0:T(8,128)(2,1)}, u32[]{:S(2)}) copy-start(bf16[128,512]{1,0:T(8,128)(2,1)} %values.3) | copy-start | bytes 393220
  15.9 28.2 %copy-start.6 = (bf16[128,512]{1,0:T(8,128)(2,1)S(1)}, bf16[128,512]{1,0:T(8,128)(2,1)}, u32[]{:S(2)}) copy-start(bf16[128,512]{1,0:T(8,128)(2,1)} %upstream.3) | copy-start | bytes 393220
  35.7 16.9 %all-to-all-start.2 = ((bf16[16,8,512]{2,1,0:T(8,128)(2,1)}), bf16[16,8,512]{2,1,0:T(8,128)(2,1)S(1)}, u32[]{:S(2)}, u32[]{:S(2)}) async-start(bf16[16,8,512]{2,1,0:T(8,128)(2,1)} %shard_map.123), calls=%async_computation.2 | async-start | bytes 262144 | tf_op jit(solution)/shard_map/all_to_all | solution.py:258

commit v2 on v1

--- a/solution.py
+++ b/solution.py
@@ -11,6 +11,7 @@
 
 VMEM = 48 * 1024 * 1024
 PARTS = 2
+GROUP = 4
 f32, bf16 = jnp.float32, jnp.bfloat16
 
 
@@ -133,7 +134,21 @@
     forward_part(load, twist, matrix, spectrum, width, outer)
 
 
-def mix_kernel(received, taps_values, twist, forward, backward, result, work):
+def swap_groups(parts):
+    lane = lax.broadcasted_iota(jnp.int32, parts[0].shape, 1)
+    low, even = lane < 64, lane // 32 % 2 == 0
+    p0, p1, p2, p3 = parts
+    p0, p2 = jnp.where(low, p0, pltpu.roll(p2, 64, 1)), jnp.where(low, pltpu.roll(p0, 64, 1), p2)
+    p1, p3 = jnp.where(low, p1, pltpu.roll(p3, 64, 1)), jnp.where(low, pltpu.roll(p1, 64, 1), p3)
+    p0, p1 = jnp.where(even, p0, pltpu.roll(p1, 32, 1)), jnp.where(even, pltpu.roll(p0, 96, 1), p1)
+    p2, p3 = jnp.where(even, p2, pltpu.roll(p3, 32, 1)), jnp.where(even, pltpu.roll(p2, 96, 1), p3)
+    return p0, p1, p2, p3
+
+
+def mix_kernel(
+    received, taps_values, twist, forward, backward,
+    lag_send, near0, near1, near2, near3, work, result, lags, turned,
+):
     blocks, width, outer = received.shape[0], received.shape[1] // 2, received.shape[2]
     for s in range(2):
         forward_part(
@@ -148,10 +163,10 @@
         hr, hi = taps_values[at, :outer], taps_values[at, outer:]
         filtered = jnp.concatenate([hr * pr - hi * pi, hr * pi + hi * pr], 1)
         mixed = jnp.concatenate([cr * hr + ci * hi, ci * hr - cr * hi], 1)
-        lags = jnp.concatenate([cr * pr + ci * pi, ci * pr - cr * pi], 1)
+        lagged = jnp.concatenate([cr * pr + ci * pi, ci * pr - cr * pi], 1)
         work[0, at, :] = accurate_dot(filtered, backward)
         work[1, at, :] = accurate_dot(mixed, backward)
-        work[2, at, :] = accurate_dot(lags, backward)
+        work[2, at, :] = accurate_dot(lagged, backward)
     norm_factor = (blocks * outer) ** -0.5
     for s in range(3):
         for g in range(width // 16):
@@ -163,36 +178,59 @@
                 values.append((re * cr + im * ci, im * cr - re * ci))
             for i, x in enumerate(interpolate(values, math.pi / 2, True)):
                 if s == 2:
-                    x = x * norm_factor
-                result[i, s * width + 16 * g : s * width + 16 * g + 16, :] = x.astype(bf16)
-
-
-def lags_kernel(back, lags):
-    width = back.shape[1] // 3
-    part = back[:, 2 * width :, :].astype(f32)
-    turned = part.reshape(part.shape[0] * width, part.shape[2]).T
-    lags[...] = turned.reshape(lags.shape).astype(bf16)
-
-
-def gates_kernel(back, out_gate, in_gate, values, upstream, mixed_out, d_out_gate, d_in_gate, d_values):
-    width = back.shape[1] // 3
-    rows = back.shape[2]
-
-    def part(s):
-        x = back[:, s * width : (s + 1) * width, :].astype(f32)
-        return x.reshape(x.shape[0] * width, rows).T
-
-    filtered, grad_mixed = part(0), part(1)
-    mixed_out[...] = (out_gate[...].astype(f32) * filtered).astype(bf16)
-    d_out_gate[...] = (upstream[...].astype(f32) * filtered).astype(bf16)
-    d_in_gate[...] = (grad_mixed * values[...].astype(f32)).astype(bf16)
-    d_values[...] = (grad_mixed * in_gate[...].astype(f32)).astype(bf16)
-
-
-def join_kernel(arrived, grad_filter):
-    span = arrived.shape[2]
-    for j in range(arrived.shape[0]):
-        grad_filter[:, j * span : (j + 1) * span] = arrived[j].astype(f32)
+                    lags[i * width + 16 * g : i * width + 16 * g + 16, :] = x * norm_factor
+                else:
+                    result[i, s * width + 16 * g : s * width + 16 * g + 16, :] = x.astype(bf16)
+    for m in range(blocks // GROUP):
+        turned[m] = lags[m * 128 : (m + 1) * 128, :].T
+        quarters = [turned[m, pl.ds(n, outer // GROUP, stride=GROUP), :] for n in range(GROUP)]
+        for n, x in enumerate(swap_groups(quarters)):
+            row = (m * GROUP + n) * (outer // GROUP)
+            lag_send[row : row + outer // GROUP, :] = x.astype(bf16)
+    place = lax.rem(lax.axis_index("ctx"), GROUP)
+    for d, near in enumerate((near0, near1, near2, near3)):
+        for x in range(GROUP):
+            near[x] = result[GROUP * x + (place ^ d)]
+
+
+def gates_kernel(
+    far0, far1, far2, far3, out_gate, in_gate, values, upstream,
+    mixed_out, d_out_gate, d_in_gate, d_values,
+):
+    width = far0.shape[1] // 2
+    span = GROUP * width
+    me = lax.axis_index("ctx")
+    column, place = lax.div(me, GROUP), lax.rem(me, GROUP)
+    for d, far in enumerate((far0, far1, far2, far3)):
+        first = pl.multiple_of(lax.rem(column + GROUP - d, GROUP) * span, span)
+        at = pl.ds(first, span)
+
+        def part(s):
+            x = [far[place ^ h, s * width : (s + 1) * width, :] for h in range(GROUP)]
+            return jnp.concatenate(x, 0).astype(f32).T
+
+        filtered, grad_mixed = part(0), part(1)
+        mixed_out[:, at] = (out_gate[:, at].astype(f32) * filtered).astype(bf16)
+        d_out_gate[:, at] = (upstream[:, at].astype(f32) * filtered).astype(bf16)
+        d_in_gate[:, at] = (grad_mixed * values[:, at].astype(f32)).astype(bf16)
+        d_values[:, at] = (grad_mixed * in_gate[:, at].astype(f32)).astype(bf16)
+
+
+def join_kernel(arrived, grad_filter, turned):
+    quads, lag_rows = turned.shape[0], grad_filter.shape[0]
+    channels = quads * 128
+    owners = grad_filter.shape[1] // channels
+    count = owners * lag_rows // GROUP
+    for m in range(quads):
+        quarters = []
+        for n in range(GROUP):
+            row = (m * GROUP + n) * count
+            quarters.append(arrived[row : row + count, :].astype(f32))
+        for n, x in enumerate(swap_groups(quarters)):
+            turned[m, pl.ds(n, count, stride=GROUP), :] = x
+        for j in range(owners):
+            first = j * channels + m * 128
+            grad_filter[:, first : first + 128] = turned[m, j * lag_rows : (j + 1) * lag_rows, :]
 
 
 def call(kernel, outs, *args, flops=1000000, vmem=VMEM, **kwargs):
@@ -247,18 +285,42 @@
             scratch_shapes=[pltpu.VMEM((blocks, 128, rows), f32)],
         ),
     )
-    result = call(
+    chunk = shape((GROUP, 2 * width, rows), bf16)
+    lag_send, *near = call(
         mix_kernel,
-        shape((blocks, 3 * width, rows), bf16),
+        (shape((blocks * rows // GROUP, 128), bf16),) + (chunk,) * GROUP,
         received, taps_values, twist, forward, backward,
-        scratch_shapes=[pltpu.VMEM((3, blocks * width, 2 * rows), f32)],
-    )
-    back = lax.all_to_all(result, "ctx", 0, 0, tiled=True)
-    lags = call(lags_kernel, shape((owners, rows // owners, channels), bf16), back)
-    arrived = lax.all_to_all(lags, "ch", 0, 0, tiled=True)
+        scratch_shapes=[
+            pltpu.VMEM((3, blocks * width, 2 * rows), f32),
+            pltpu.VMEM((blocks, 2 * width, rows), bf16),
+            pltpu.VMEM((blocks * width, rows), f32),
+            pltpu.VMEM((blocks // GROUP, rows, 128), f32),
+        ],
+    )
+    lag_rows = rows // owners
+    chunks = lag_send.reshape(blocks * owners, lag_rows // GROUP, 128)
+    arrived = lax.all_to_all(chunks, ("ctx", "ch"), 0, 0, tiled=True).reshape(lag_send.shape)
+
+    near = near[:1] + [
+        lax.ppermute(near[d], "ctx", [(i, i ^ d) for i in range(blocks)]) for d in range(1, GROUP)
+    ]
+    near = jnp.stack(near)
+    far = [
+        lax.dynamic_index_in_dim(near, (me // GROUP + d) % GROUP, 1, keepdims=False)
+        for d in range(GROUP)
+    ]
+    far = far[:1] + [
+        lax.ppermute(far[d], "ctx", [(i, (i + GROUP * d) % blocks) for i in range(blocks)])
+        for d in range(1, GROUP)
+    ]
     out = shape((rows, channels), bf16)
-    gates = call(gates_kernel, (out,) * 4, back, out_gate, in_gate, values, upstream)
-    grad_filter = call(join_kernel, shape((rows // owners, owners * channels), f32), arrived)
+    gates = call(gates_kernel, (out,) * 4, *far, out_gate, in_gate, values, upstream)
+    grad_filter = call(
+        join_kernel,
+        shape((lag_rows, owners * channels), f32),
+        arrived,
+        scratch_shapes=[pltpu.VMEM((channels // 128, rows, 128), f32)],
+    )
     return (*gates, grad_filter)
 
 

time: 53.8 us -> 50.7 us (0.942)
  blocking collectives: 13 us -> 0 us
  starting transfers between devices: 17 us -> 27.4 us
  waiting for transfers between devices: 11.8 us -> 10.8 us
    all_to_all x1 -> x0, blocking collectives: 13 us -> none  [body(): back = lax.all_to_all(result, 'ctx', 0, 0, tiled=True)]
    ppermute x0 -> x6, starting transfers between devices: none -> 8.68 us  [the longest x3 5.04 us: body(): lax.ppermute(far[d], 'ctx', [(i, (i + GROUP * d) % blocks) for i in range...]
    all_to_all x1, waiting for transfers between devices: 7.53 us -> 3.77 us  [body(): lax.all_to_all(chunks, ('ctx', 'ch'), 0, 0, tiled=True)]
    ppermute x0 -> x6, waiting for transfers between devices: none -> 2.76 us  [the longest x3 2.76 us: body(): lax.ppermute(far[d], 'ctx', [(i, (i + GROUP * d) % blocks) for i in range...]
    all_to_all x1, starting transfers between devices: 8.4 us -> 10.1 us  [body(): lax.all_to_all(chunks, ('ctx', 'ch'), 0, 0, tiled=True)]
    pallas_call x6 -> x5, Pallas kernels: 7.42 us -> 7.94 us  [call(): pl.pallas_call(kernel, out_shape=outs, compiler_params=pltpu.CompilerPara...]
  transfers between devices with their start and end apart: 2 -> 8, of which waited for: 2 -> 3; matrix products, arithmetic and copies ran while one was open for 0% -> 0% of each run, Pallas kernels for 4% -> 4%
where the time goes in v2:
time: 50.7 us; the launch traced here: 50.4 us
  starting transfers between devices  27.4 us (54%)
  waiting for transfers between devices  10.8 us (21%)
  Pallas kernels  7.94 us (16%)
  local copies, waits for them, and re-layouts  3.33 us (7%)
  between operations  0.78 us (2%)
    all_to_all x1, starting transfers between devices, body(): lax.all_to_all(chunks, ('ctx', 'ch'), 0, 0, tiled=True)  10.1 us
    all_to_all x1, starting transfers between devices, body(): received = lax.all_to_all(send, 'ctx', 0, 0, tiled=True)  8.59 us
    pallas_call x5, Pallas kernels, call(): pl.pallas_call(kernel, out_shape=outs, compiler_params=pltpu.CompilerPara...  7.94 us
    ppermute x3, starting transfers between devices, body(): lax.ppermute(far[d], 'ctx', [(i, (i + GROUP * d) % blocks) for i in range...  5.04 us
    all_to_all x1, waiting for transfers between devices, body(): received = lax.all_to_all(send, 'ctx', 0, 0, tiled=True)  4.24 us
    all_to_all x1, waiting for transfers between devices, body(): lax.all_to_all(chunks, ('ctx', 'ch'), 0, 0, tiled=True)  3.77 us
    ppermute x3, starting transfers between devices, body(): lax.ppermute(near[d], 'ctx', [(i, i ^ d) for i in range(blocks)])  3.64 us
    unnamed x20, local copies, waits for them, and re-layouts  3.3 us
  transfers between devices with their start and end apart: 8, of which 3 were waited for; matrix products, arithmetic and copies ran while one was open for 0% of the time, Pallas kernels for 4%

profile of v2, /device:TPU:1, one launch (start us, length us, event | category | flops | bytes accessed | tf_op | source)
XLA Modules:
  0.0 50.4 jit_solution(1350736650700390546)
XLA Ops:
  0.6 2.0 %shard_map.119 = bf16[16,64,128]{2,1,0:T(8,128)(2,1)} custom-call(bf16[128,512]{1,0:T(8,128)(2,1)} %out_gate.3, bf16[128,512]{1,0:T(8,128)(2,1)} %in_gate.3, bf16[128,512]{1,0:T(8,128)(2,1)} %values.3, bf16[128,512]{1,0:T(8,128)(2,1)} %upstream.3), custom_call_target="tpu_custom_call" | custom-call | flops 1000000 | bytes 1048576 | tf_op jit(solution)/shard_map/pallas_call | solution.py:237
  2.6 0.0 copy-start.2
  2.6 0.0 copy-start.7
  2.6 0.0 copy-start.9
  2.6 8.6 %all-to-all-start = ((bf16[16,64,128]{2,1,0:T(8,128)(2,1)}), bf16[16,64,128]{2,1,0:T(8,128)(2,1)S(1)}, u32[]{:S(2)}, u32[]{:S(2)}) async-start(bf16[16,64,128]{2,1,0:T(8,128)(2,1)} %shard_map.119), calls=%async_computation | async-start | bytes 524288 | tf_op jit(solution)/shard_map/all_to_all | solution.py:266
  11.2 0.1 pad_add_fusion.index
  11.3 1.6 %copy-done = bf16[2048,512]{1,0:T(8,128)(2,1)S(1)} copy-done((bf16[2048,512]{1,0:T(8,128)(2,1)S(1)}, bf16[2048,512]{1,0:T(8,128)(2,1)}, u32[]{:S(2)}) %copy-start) | copy-done | bytes 2097176
  12.9 0.9 %copy-done.1 = bf16[2,256,256]{2,1,0:T(8,128)(2,1)S(1)} copy-done((bf16[2,256,256]{2,1,0:T(8,128)(2,1)S(1)}, bf16[2,256,256]{2,1,0:T(8,128)(2,1)}, u32[]{:S(2)}) %copy-start.1) | copy-done | bytes 262168
  13.8 0.7 %copy-done.8 = f32[32,128]{1,0:T(8,128)S(1)} copy-done((f32[32,128]{1,0:T(8,128)S(1)}, f32[32,128]{1,0:T(8,128)}, u32[]{:S(2)}) %copy-start.8) | copy-done | bytes 16408
  14.6 1.3 %shard_map.120.taps_values = f32[512,256]{1,0:T(8,128)S(1)} custom-call(s32[2]{0:T(128)S(1)} %pad_add_fusion.index, bf16[2048,512]{1,0:T(8,128)(2,1)S(1)} %copy-done, f32[32,128]{1,0:T(8,128)S(1)} %copy-done.8, bf16[2,256,256]{2,1,0:T(8,128)(2,1)S(1)} %copy-done.1), custom_call_target="tpu_custom_call" | custom-call | flops 1000000 | bytes 1048576 | tf_op jit(solution)/shard_map/pallas_call | solution.py:237
  15.9 0.0 copy-start.5
  15.9 4.2 %all-to-all-done.received = bf16[16,64,128]{2,1,0:T(8,128)(2,1)S(1)} async-done(((bf16[16,64,128]{2,1,0:T(8,128)(2,1)}), bf16[16,64,128]{2,1,0:T(8,128)(2,1)S(1)}, u32[]{:S(2)}, u32[]{:S(2)}) %all-to-all-start) | async-done | bytes 262176 | tf_op jit(solution)/shard_map/all_to_all | solution.py:266
  20.1 2.8 %shard_map.121 = (bf16[512,128]{1,0:T(8,128)(2,1)}, bf16[4,64,128]{2,1,0:T(8,128)(2,1)S(1)}, bf16[4,64,128]{2,1,0:T(8,128)(2,1)S(1)}, bf16[4,64,128]{2,1,0:T(8,128)(2,1)S(1)}, bf16[4,64,128]{2,1,0:T(8,128)(2,1)S(1)}) custom-call(bf16[16,64,128]{2,1,0:T(8,128)(2,1)S(1)} %all-to-all-done.received, f32[512,256]{1,0:T(8,128)S(1)} %shard_map.120.taps_values, ...), custom_call_target="tpu_custom_call" | custom-call | flops 1000000 | bytes 1048576 | tf_op jit(solution)/shard_map/pallas_call | solution.py:237
  22.9 0.7 %collective-permute-start.2 = (bf16[4,64,128]{2,1,0:T(8,128)(2,1)S(1)}, bf16[4,64,128]{2,1,0:T(8,128)(2,1)S(1)}, u32[]{:S(2)}, u32[]{:S(2)}) collective-permute-start(bf16[4,64,128]{2,1,0:T(8,128)(2,1)S(1)} %get-tuple-element.17), channel_id=1, source_target_pairs={{0,48},{16,32},{32,16},{48,0},{64,112},{80,96},{96,80},{112,64},{1... | collective-permute-start | bytes 196616 | tf_op jit(solution)/shard_map/ppermute | solution.py:305
  23.7 2.6 %collective-permute-start.1 = (bf16[4,64,128]{2,1,0:T(8,128)(2,1)S(1)}, bf16[4,64,128]{2,1,0:T(8,128)(2,1)S(1)}, u32[]{:S(2)}, u32[]{:S(2)}) collective-permute-start(bf16[4,64,128]{2,1,0:T(8,128)(2,1)S(1)} %get-tuple-element.16), channel_id=1, source_target_pairs={{0,32},{16,48},{32,0},{48,16},{64,96},{80,112},{96,64},{112,80},{1... | collective-permute-start | bytes 196616 | tf_op jit(solution)/shard_map/ppermute | solution.py:305
  26.2 0.4 collective-permute-start
  26.6 10.1 %all-to-all-start.1 = ((bf16[256,2,128]{2,1,0:T(2,128)(2,1)}), bf16[256,2,128]{2,1,0:T(2,128)(2,1)S(1)}, u32[]{:S(2)}, u32[]{:S(2)}) async-start(bf16[256,2,128]{2,1,0:T(2,128)(2,1)} %bitcast.10), calls=%async_computation.1 | async-start | bytes 262144 | tf_op jit(solution)/shard_map/all_to_all | solution.py:302
  36.8 1.5 %collective-permute-start.3 = (bf16[4,64,128]{2,1,0:T(8,128)(2,1)S(1)}, bf16[4,64,128]{2,1,0:T(8,128)(2,1)S(1)}, u32[]{:S(2)}, u32[]{:S(2)}) collective-permute-start(bf16[4,64,128]{2,1,0:T(8,128)(2,1)S(1)} %get-tuple-element.25), channel_id=1, source_target_pairs={{0,64},{16,80},{32,96},{48,112},{64,128},{80,144},{96,160},{112,17... | collective-permute-start | bytes 196616 | tf_op jit(solution)/shard_map/ppermute | solution.py:313
  38.3 2.4 %collective-permute-start.4 = (bf16[4,64,128]{2,1,0:T(8,128)(2,1)S(1)}, bf16[4,64,128]{2,1,0:T(8,128)(2,1)S(1)}, u32[]{:S(2)}, u32[]{:S(2)}) collective-permute-start(bf16[4,64,128]{2,1,0:T(8,128)(2,1)S(1)} %get-tuple-element.24), channel_id=1, source_target_pairs={{0,128},{16,144},{32,160},{48,176},{64,192},{80,208},{96,224},{112... | collective-permute-start | bytes 196616 | tf_op jit(solution)/shard_map/ppermute | solution.py:313
  40.7 1.2 %collective-permute-start.5 = (bf16[4,64,128]{2,1,0:T(8,128)(2,1)S(1)}, bf16[4,64,128]{2,1,0:T(8,128)(2,1)S(1)}, u32[]{:S(2)}, u32[]{:S(2)}) collective-permute-start(bf16[4,64,128]{2,1,0:T(8,128)(2,1)S(1)} %get-tuple-element.23), channel_id=1, source_target_pairs={{0,192},{16,208},{32,224},{48,240},{64,0},{80,16},{96,32},{112,48}... | collective-permute-start | bytes 196616 | tf_op jit(solution)/shard_map/ppermute | solution.py:313
  41.9 2.8 %collective-permute-done.4.far2 = bf16[4,64,128]{2,1,0:T(8,128)(2,1)S(1)} collective-permute-done((bf16[4,64,128]{2,1,0:T(8,128)(2,1)S(1)}, bf16[4,64,128]{2,1,0:T(8,128)(2,1)S(1)}, u32[]{:S(2)}, u32[]{:S(2)}) %collective-permute-start.4) | collective-permute-done | bytes 65568 | tf_op jit(solution)/shard_map/ppermute | solution.py:313
  44.7 1.0 %shard_map.122 = (bf16[128,512]{1,0:T(8,128)(2,1)}, bf16[128,512]{1,0:T(8,128)(2,1)}, bf16[128,512]{1,0:T(8,128)(2,1)}, bf16[128,512]{1,0:T(8,128)(2,1)}) custom-call(bf16[4,64,128]{2,1,0:T(8,128)(2,1)S(1)} %get-tuple-element.26.far0, bf16[4,64,128]{2,1,0:T(8,128)(2,1)S(1)} %collective-permute-done.3.far1, ...), custom_call_target="tpu_custom_call" | custom-call | flops 1000000 | bytes 1048576 | tf_op jit(solution)/shard_map/pallas_call | solution.py:237
  45.7 3.8 %all-to-all-done.1 = bf16[256,2,128]{2,1,0:T(2,128)(2,1)S(1)} async-done(((bf16[256,2,128]{2,1,0:T(2,128)(2,1)}), bf16[256,2,128]{2,1,0:T(2,128)(2,1)S(1)}, u32[]{:S(2)}, u32[]{:S(2)}) %all-to-all-start.1) | async-done | bytes 131104 | tf_op jit(solution)/shard_map/all_to_all | solution.py:302
  49.4 0.9 %shard_map.123 = f32[8,8192]{1,0:T(8,128)} custom-call(bf16[512,128]{1,0:T(8,128)(2,1)S(1)} %bitcast.16), custom_call_target="tpu_custom_call" | custom-call | flops 1000000 | bytes 1048576 | tf_op jit(solution)/shard_map/pallas_call | solution.py:237
  (20 shorter events, 0.1 us)
Async XLA Ops:
  2.6 17.5 %copy-start.2 = (bf16[2,256,256]{2,1,0:T(8,128)(2,1)S(1)}, bf16[2,256,256]{2,1,0:T(8,128)(2,1)}, u32[]{:S(2)}) copy-start(bf16[2,256,256]{2,1,0:T(8,128)(2,1)} %constant.90.clone.matrix.forward) | copy-start | bytes 786436
  2.6 17.5 %copy-start.7 = (bf16[2,256,256]{2,1,0:T(8,128)(2,1)S(1)}, bf16[2,256,256]{2,1,0:T(8,128)(2,1)}, u32[]{:S(2)}) copy-start(bf16[2,256,256]{2,1,0:T(8,128)(2,1)} %constant.91.clone.backward) | copy-start | bytes 786436
  2.6 17.5 %copy-start.9 = (f32[32,128]{1,0:T(8,128)S(1)}, f32[32,128]{1,0:T(8,128)}, u32[]{:S(2)}) copy-start(f32[32,128]{1,0:T(8,128)} %constant.89.clone.twist) | copy-start | bytes 49156
  2.6 17.5 %all-to-all-start = ((bf16[16,64,128]{2,1,0:T(8,128)(2,1)}), bf16[16,64,128]{2,1,0:T(8,128)(2,1)S(1)}, u32[]{:S(2)}, u32[]{:S(2)}) async-start(bf16[16,64,128]{2,1,0:T(8,128)(2,1)} %shard_map.119), calls=%async_computation | async-start | bytes 524288 | tf_op jit(solution)/shard_map/all_to_all | solution.py:266
  11.3 1.6 %copy-start = (bf16[2048,512]{1,0:T(8,128)(2,1)S(1)}, bf16[2048,512]{1,0:T(8,128)(2,1)}, u32[]{:S(2)}) copy-start(bf16[2048,512]{1,0:T(8,128)(2,1)} %taps.1) | copy-start | bytes 6291460
  12.9 0.9 %copy-start.1 = (bf16[2,256,256]{2,1,0:T(8,128)(2,1)S(1)}, bf16[2,256,256]{2,1,0:T(8,128)(2,1)}, u32[]{:S(2)}) copy-start(bf16[2,256,256]{2,1,0:T(8,128)(2,1)} %constant.90.clone.matrix.forward) | copy-start | bytes 786436
  13.8 0.7 %copy-start.8 = (f32[32,128]{1,0:T(8,128)S(1)}, f32[32,128]{1,0:T(8,128)}, u32[]{:S(2)}) copy-start(f32[32,128]{1,0:T(8,128)} %constant.89.clone.twist) | copy-start | bytes 49156
  15.8 28.8 %copy-start.3 = (bf16[128,512]{1,0:T(8,128)(2,1)S(1)}, bf16[128,512]{1,0:T(8,128)(2,1)}, u32[]{:S(2)}) copy-start(bf16[128,512]{1,0:T(8,128)(2,1)} %out_gate.3) | copy-start | bytes 393220
  15.8 28.8 %copy-start.4 = (bf16[128,512]{1,0:T(8,128)(2,1)S(1)}, bf16[128,512]{1,0:T(8,128)(2,1)}, u32[]{:S(2)}) copy-start(bf16[128,512]{1,0:T(8,128)(2,1)} %in_gate.3) | copy-start | bytes 393220
  15.9 28.8 %copy-start.5 = (bf16[128,512]{1,0:T(8,128)(2,1)S(1)}, bf16[128,512]{1,0:T(8,128)(2,1)}, u32[]{:S(2)}) copy-start(bf16[128,512]{1,0:T(8,128)(2,1)} %values.3) | copy-start | bytes 393220
  15.9 28.8 %copy-start.6 = (bf16[128,512]{1,0:T(8,128)(2,1)S(1)}, bf16[128,512]{1,0:T(8,128)(2,1)}, u32[]{:S(2)}) copy-start(bf16[128,512]{1,0:T(8,128)(2,1)} %upstream.3) | copy-start | bytes 393220
  22.9 13.8 %collective-permute-start.2 = (bf16[4,64,128]{2,1,0:T(8,128)(2,1)S(1)}, bf16[4,64,128]{2,1,0:T(8,128)(2,1)S(1)}, u32[]{:S(2)}, u32[]{:S(2)}) collective-permute-start(bf16[4,64,128]{2,1,0:T(8,128)(2,1)S(1)} %get-tuple-element.17), channel_id=1, source_target_pairs={{0,48},{16,32},{32,16},{48,0},{64,112},{80,96},{96,80},{112,64},{1... | collective-permute-start | bytes 196616 | tf_op jit(solution)/shard_map/ppermute | solution.py:305
  23.7 13.1 %collective-permute-start.1 = (bf16[4,64,128]{2,1,0:T(8,128)(2,1)S(1)}, bf16[4,64,128]{2,1,0:T(8,128)(2,1)S(1)}, u32[]{:S(2)}, u32[]{:S(2)}) collective-permute-start(bf16[4,64,128]{2,1,0:T(8,128)(2,1)S(1)} %get-tuple-element.16), channel_id=1, source_target_pairs={{0,32},{16,48},{32,0},{48,16},{64,96},{80,112},{96,64},{112,80},{1... | collective-permute-start | bytes 196616 | tf_op jit(solution)/shard_map/ppermute | solution.py:305
  26.2 10.5 %collective-permute-start = (bf16[4,64,128]{2,1,0:T(8,128)(2,1)S(1)}, bf16[4,64,128]{2,1,0:T(8,128)(2,1)S(1)}, u32[]{:S(2)}, u32[]{:S(2)}) collective-permute-start(bf16[4,64,128]{2,1,0:T(8,128)(2,1)S(1)} %get-tuple-element.15), channel_id=1, source_target_pairs={{0,16},{16,0},{32,48},{48,32},{64,80},{80,64},{96,112},{112,96},{1... | collective-permute-start | bytes 196616 | tf_op jit(solution)/shard_map/ppermute | solution.py:305
  26.6 22.8 %all-to-all-start.1 = ((bf16[256,2,128]{2,1,0:T(2,128)(2,1)}), bf16[256,2,128]{2,1,0:T(2,128)(2,1)S(1)}, u32[]{:S(2)}, u32[]{:S(2)}) async-start(bf16[256,2,128]{2,1,0:T(2,128)(2,1)} %bitcast.10), calls=%async_computation.1 | async-start | bytes 262144 | tf_op jit(solution)/shard_map/all_to_all | solution.py:302
  36.8 5.0 %collective-permute-start.3 = (bf16[4,64,128]{2,1,0:T(8,128)(2,1)S(1)}, bf16[4,64,128]{2,1,0:T(8,128)(2,1)S(1)}, u32[]{:S(2)}, u32[]{:S(2)}) collective-permute-start(bf16[4,64,128]{2,1,0:T(8,128)(2,1)S(1)} %get-tuple-element.25), channel_id=1, source_target_pairs={{0,64},{16,80},{32,96},{48,112},{64,128},{80,144},{96,160},{112,17... | collective-permute-start | bytes 196616 | tf_op jit(solution)/shard_map/ppermute | solution.py:313
  38.3 6.3 %collective-permute-start.4 = (bf16[4,64,128]{2,1,0:T(8,128)(2,1)S(1)}, bf16[4,64,128]{2,1,0:T(8,128)(2,1)S(1)}, u32[]{:S(2)}, u32[]{:S(2)}) collective-permute-start(bf16[4,64,128]{2,1,0:T(8,128)(2,1)S(1)} %get-tuple-element.24), channel_id=1, source_target_pairs={{0,128},{16,144},{32,160},{48,176},{64,192},{80,208},{96,224},{112... | collective-permute-start | bytes 196616 | tf_op jit(solution)/shard_map/ppermute | solution.py:313
  40.7 3.9 %collective-permute-start.5 = (bf16[4,64,128]{2,1,0:T(8,128)(2,1)S(1)}, bf16[4,64,128]{2,1,0:T(8,128)(2,1)S(1)}, u32[]{:S(2)}, u32[]{:S(2)}) collective-permute-start(bf16[4,64,128]{2,1,0:T(8,128)(2,1)S(1)} %get-tuple-element.23), channel_id=1, source_target_pairs={{0,192},{16,208},{32,224},{48,240},{64,0},{80,16},{96,32},{112,48}... | collective-permute-start | bytes 196616 | tf_op jit(solution)/shard_map/ppermute | solution.py:313

commit v3 on v2

--- a/solution.py
+++ b/solution.py
@@ -83,7 +83,7 @@
     return dot(top, m_ref[0]) + (dot(rest, m_ref[0]) + dot(top, m_ref[1]))
 
 
-def send_kernel(out_gate, in_gate, values, upstream, send, held, arrived):
+def send_kernel(out_gate, in_gate, values, upstream, send, held, arrived, ready, sent):
     blocks, width = send.shape[0], send.shape[1] // 2
     rows, channels = out_gate.shape
     part = channels // PARTS
@@ -92,6 +92,10 @@
     def fetch(n, p):
         at = slice(p * part, (p + 1) * part)
         return pltpu.make_async_copy(sources[n].at[:, at], held.at[n, p], arrived.at[n, p])
+
+    def leave(p):
+        at = slice(p * part // width, (p + 1) * part // width)
+        return pltpu.make_async_copy(ready.at[at], send.at[at], sent.at[p])
 
     for p in range(PARTS):
         for n in range(4):
@@ -102,9 +106,12 @@
             fetch(2 * s, p).wait()
             fetch(2 * s + 1, p).wait()
             gated = (held[2 * s, p].astype(f32) * held[2 * s + 1, p].astype(f32)).astype(bf16)
-            send[first : first + part // width, s * width : (s + 1) * width, :] = gated.T.reshape(
+            ready[first : first + part // width, s * width : (s + 1) * width, :] = gated.T.reshape(
                 part // width, width, rows
             )
+        leave(p).start()
+    for p in range(PARTS):
+        leave(p).wait()
 
 
 def forward_part(load, twist, matrix, work, width, outer):
@@ -147,7 +154,7 @@
 
 def mix_kernel(
     received, taps_values, twist, forward, backward,
-    lag_send, near0, near1, near2, near3, work, result, lags, turned,
+    lag_send, near0, near1, work, result, lags, turned, packed, done,
 ):
     blocks, width, outer = received.shape[0], received.shape[1] // 2, received.shape[2]
     for s in range(2):
@@ -168,7 +175,7 @@
         work[1, at, :] = accurate_dot(mixed, backward)
         work[2, at, :] = accurate_dot(lagged, backward)
     norm_factor = (blocks * outer) ** -0.5
-    for s in range(3):
+    def inverse(s, store):
         for g in range(width // 16):
             values = []
             for k in range(blocks):
@@ -177,20 +184,44 @@
                 re, im = work[s, at, :outer], work[s, at, outer:]
                 values.append((re * cr + im * ci, im * cr - re * ci))
             for i, x in enumerate(interpolate(values, math.pi / 2, True)):
-                if s == 2:
-                    lags[i * width + 16 * g : i * width + 16 * g + 16, :] = x * norm_factor
-                else:
-                    result[i, s * width + 16 * g : s * width + 16 * g + 16, :] = x.astype(bf16)
+                store(i, slice(16 * g, 16 * g + 16), x)
+
+    def keep_lags(i, at, x):
+        lags[i * width + at.start : i * width + at.stop, :] = x * norm_factor
+
+    inverse(2, keep_lags)
     for m in range(blocks // GROUP):
         turned[m] = lags[m * 128 : (m + 1) * 128, :].T
         quarters = [turned[m, pl.ds(n, outer // GROUP, stride=GROUP), :] for n in range(GROUP)]
         for n, x in enumerate(swap_groups(quarters)):
             row = (m * GROUP + n) * (outer // GROUP)
-            lag_send[row : row + outer // GROUP, :] = x.astype(bf16)
+            packed[row : row + outer // GROUP, :] = x.astype(bf16)
+    out = pltpu.make_async_copy(packed, lag_send, done)
+    out.start()
+
+    @pl.loop(0, 2)
+    def _(s):
+        def keep(i, at, x):
+            result[s, i, at, :] = x.astype(bf16)
+
+        inverse(s, keep)
+
     place = lax.rem(lax.axis_index("ctx"), GROUP)
-    for d, near in enumerate((near0, near1, near2, near3)):
-        for x in range(GROUP):
-            near[x] = result[GROUP * x + (place ^ d)]
+    for k, near in enumerate((near0, near1)):
+        for e in range(2):
+            for x in range(GROUP):
+                for s in range(2):
+                    source = result[s, GROUP * x + (place ^ (2 * k + e))]
+                    near[e, x, s * width : (s + 1) * width, :] = source
+    out.wait()
+
+
+def turn_kernel(stay, came, crossed, far0, far1, far2, far3):
+    column = lax.div(lax.axis_index("ctx"), GROUP)
+    for d, far in enumerate((far0, far1, far2, far3)):
+        x = lax.rem(column + d, GROUP)
+        far[0], far[1] = stay[0, x], came[0, x]
+        far[2], far[3] = crossed[0, x], crossed[1, x]
 
 
 def gates_kernel(
@@ -201,12 +232,13 @@
     span = GROUP * width
     me = lax.axis_index("ctx")
     column, place = lax.div(me, GROUP), lax.rem(me, GROUP)
+    slot = lambda e: lax.rem(e, 2) * 2 + lax.div(e, 2)
     for d, far in enumerate((far0, far1, far2, far3)):
         first = pl.multiple_of(lax.rem(column + GROUP - d, GROUP) * span, span)
         at = pl.ds(first, span)
 
         def part(s):
-            x = [far[place ^ h, s * width : (s + 1) * width, :] for h in range(GROUP)]
+            x = [far[slot(place ^ h), s * width : (s + 1) * width, :] for h in range(GROUP)]
             return jnp.concatenate(x, 0).astype(f32).T
 
         filtered, grad_mixed = part(0), part(1)
@@ -261,7 +293,10 @@
         scratch_shapes=[
             pltpu.VMEM((4, PARTS, rows, channels // PARTS), bf16),
             pltpu.SemaphoreType.DMA((4, PARTS)),
+            pltpu.VMEM((blocks, 2 * width, rows), bf16),
+            pltpu.SemaphoreType.DMA((PARTS,)),
         ],
+        out_specs=pl.BlockSpec(memory_space=pltpu.HBM),
     )
     received = lax.all_to_all(send, "ctx", 0, 0, tiled=True)
 
@@ -285,36 +320,37 @@
             scratch_shapes=[pltpu.VMEM((blocks, 128, rows), f32)],
         ),
     )
-    chunk = shape((GROUP, 2 * width, rows), bf16)
-    lag_send, *near = call(
+    near = shape((2, GROUP, 2 * width, rows), bf16)
+    lag_send, stay, leave = call(
         mix_kernel,
-        (shape((blocks * rows // GROUP, 128), bf16),) + (chunk,) * GROUP,
+        (shape((blocks * rows // GROUP, 128), bf16), near, near),
         received, taps_values, twist, forward, backward,
         scratch_shapes=[
             pltpu.VMEM((3, blocks * width, 2 * rows), f32),
-            pltpu.VMEM((blocks, 2 * width, rows), bf16),
+            pltpu.VMEM((2, blocks, width, rows), bf16),
             pltpu.VMEM((blocks * width, rows), f32),
             pltpu.VMEM((blocks // GROUP, rows, 128), f32),
+            pltpu.VMEM((blocks * rows // GROUP, 128), bf16),
+            pltpu.SemaphoreType.DMA,
         ],
+        out_specs=(pl.BlockSpec(memory_space=pltpu.HBM),) + (pl.BlockSpec(memory_space=pltpu.VMEM),) * 2,
     )
     lag_rows = rows // owners
     chunks = lag_send.reshape(blocks * owners, lag_rows // GROUP, 128)
     arrived = lax.all_to_all(chunks, ("ctx", "ch"), 0, 0, tiled=True).reshape(lag_send.shape)
 
-    near = near[:1] + [
-        lax.ppermute(near[d], "ctx", [(i, i ^ d) for i in range(blocks)]) for d in range(1, GROUP)
-    ]
-    near = jnp.stack(near)
-    far = [
-        lax.dynamic_index_in_dim(near, (me // GROUP + d) % GROUP, 1, keepdims=False)
-        for d in range(GROUP)
-    ]
+    came = lax.ppermute(leave, "ctx", [(i, i ^ 2) for i in range(blocks)])
+    cross = jnp.stack([stay[1], came[1]])
+    crossed = lax.ppermute(cross, "ctx", [(i, i ^ 1) for i in range(blocks)])
+    far = call(turn_kernel, (shape((GROUP, 2 * width, rows), bf16),) * GROUP, stay, came, crossed)
+    far = list(far)
     far = far[:1] + [
         lax.ppermute(far[d], "ctx", [(i, (i + GROUP * d) % blocks) for i in range(blocks)])
         for d in range(1, GROUP)
     ]
     out = shape((rows, channels), bf16)
     gates = call(gates_kernel, (out,) * 4, *far, out_gate, in_gate, values, upstream)
+    arrived, *gates = lax.optimization_barrier((arrived, *gates))
     grad_filter = call(
         join_kernel,
         shape((lag_rows, owners * channels), f32),

time: 50.7 us -> 49.8 us (0.982)
    all_to_all x1, starting transfers between devices: 10.1 us -> 12.5 us  [body(): lax.all_to_all(chunks, ('ctx', 'ch'), 0, 0, tiled=True)]
    all_to_all x1, waiting for transfers between devices: 3.77 us -> 1.69 us  [body(): lax.all_to_all(chunks, ('ctx', 'ch'), 0, 0, tiled=True)]
    ppermute x3, starting transfers between devices: 5.04 us -> 3.25 us  [body(): lax.ppermute(far[d], 'ctx', [(i, (i + GROUP * d) % blocks) for i in range...]
    ppermute x3 -> x2, waiting for transfers between devices: 0.01 us -> 0.99 us  [the longest x1 0.99 us: body(): crossed = lax.ppermute(cross, 'ctx', [(i, i ^ 1) for i in range(blocks)])]
    ppermute x3 -> x2, starting transfers between devices: 3.64 us -> 2.95 us  [the longest x1 2.23 us: body(): crossed = lax.ppermute(cross, 'ctx', [(i, i ^ 1) for i in range(blocks)])]
    ppermute x3, waiting for transfers between devices: 2.76 us -> 3.41 us  [body(): lax.ppermute(far[d], 'ctx', [(i, (i + GROUP * d) % blocks) for i in range...]
    pallas_call x5 -> x6, Pallas kernels: 7.94 us -> 7.6 us  [call(): pl.pallas_call(kernel, out_shape=outs, compiler_params=pltpu.CompilerPara...]
  transfers between devices with their start and end apart: 8 -> 7, of which waited for: 3 -> 4; matrix products, arithmetic and copies ran while one was open for 0% -> 0% of each run, Pallas kernels for 4% -> 5%
where the time goes in v3:
time: 49.8 us; the launch traced here: 49.5 us
  starting transfers between devices  27.3 us (55%)
  waiting for transfers between devices  10.4 us (21%)
  Pallas kernels  7.6 us (15%)
  local copies, waits for them, and re-layouts  3.3 us (7%)
  between operations  0.77 us (2%)
    all_to_all x1, starting transfers between devices, body(): lax.all_to_all(chunks, ('ctx', 'ch'), 0, 0, tiled=True)  12.5 us
    all_to_all x1, starting transfers between devices, body(): received = lax.all_to_all(send, 'ctx', 0, 0, tiled=True)  8.59 us
    pallas_call x6, Pallas kernels, call(): pl.pallas_call(kernel, out_shape=outs, compiler_params=pltpu.CompilerPara...  7.6 us
    all_to_all x1, waiting for transfers between devices, body(): received = lax.all_to_all(send, 'ctx', 0, 0, tiled=True)  4.3 us
    ppermute x3, waiting for transfers between devices, body(): lax.ppermute(far[d], 'ctx', [(i, (i + GROUP * d) % blocks) for i in range...  3.41 us
    unnamed x20, local copies, waits for them, and re-layouts  3.29 us
    ppermute x3, starting transfers between devices, body(): lax.ppermute(far[d], 'ctx', [(i, (i + GROUP * d) % blocks) for i in range...  3.25 us
    ppermute x1, starting transfers between devices, body(): crossed = lax.ppermute(cross, 'ctx', [(i, i ^ 1) for i in range(blocks)])  2.23 us
  transfers between devices with their start and end apart: 7, of which 4 were waited for; matrix products, arithmetic and copies ran while one was open for 0% of the time, Pallas kernels for 5%

profile of v3, /device:TPU:1, one launch (start us, length us, event | category | flops | bytes accessed | tf_op | source)
XLA Modules:
  0.0 49.5 jit_solution(4312483346169183651)
XLA Ops:
  0.6 1.9 %shard_map.119 = bf16[16,64,128]{2,1,0:T(8,128)(2,1)} custom-call(bf16[128,512]{1,0:T(8,128)(2,1)} %out_gate.3, bf16[128,512]{1,0:T(8,128)(2,1)} %in_gate.3, bf16[128,512]{1,0:T(8,128)(2,1)} %values.3, bf16[128,512]{1,0:T(8,128)(2,1)} %upstream.3), custom_call_target="tpu_custom_call" | custom-call | flops 1000000 | bytes 1048576 | tf_op jit(solution)/shard_map/pallas_call | solution.py:269
  2.6 0.0 copy-start.2
  2.6 0.0 copy-start.7
  2.6 0.0 copy-start.9
  2.6 8.6 %all-to-all-start = ((bf16[16,64,128]{2,1,0:T(8,128)(2,1)}), bf16[16,64,128]{2,1,0:T(8,128)(2,1)S(1)}, u32[]{:S(2)}, u32[]{:S(2)}) async-start(bf16[16,64,128]{2,1,0:T(8,128)(2,1)} %shard_map.119), calls=%async_computation | async-start | bytes 524288 | tf_op jit(solution)/shard_map/all_to_all | solution.py:301
  11.2 0.1 pad_add_fusion.index
  11.3 1.6 %copy-done = bf16[2048,512]{1,0:T(8,128)(2,1)S(1)} copy-done((bf16[2048,512]{1,0:T(8,128)(2,1)S(1)}, bf16[2048,512]{1,0:T(8,128)(2,1)}, u32[]{:S(2)}) %copy-start) | copy-done | bytes 2097176
  12.9 0.9 %copy-done.1 = bf16[2,256,256]{2,1,0:T(8,128)(2,1)S(1)} copy-done((bf16[2,256,256]{2,1,0:T(8,128)(2,1)S(1)}, bf16[2,256,256]{2,1,0:T(8,128)(2,1)}, u32[]{:S(2)}) %copy-start.1) | copy-done | bytes 262168
  13.8 0.7 %copy-done.8 = f32[32,128]{1,0:T(8,128)S(1)} copy-done((f32[32,128]{1,0:T(8,128)S(1)}, f32[32,128]{1,0:T(8,128)}, u32[]{:S(2)}) %copy-start.8) | copy-done | bytes 16408
  14.5 1.3 %shard_map.120.taps_values = f32[512,256]{1,0:T(8,128)S(1)} custom-call(s32[2]{0:T(128)S(1)} %pad_add_fusion.index, bf16[2048,512]{1,0:T(8,128)(2,1)S(1)} %copy-done, f32[32,128]{1,0:T(8,128)S(1)} %copy-done.8, bf16[2,256,256]{2,1,0:T(8,128)(2,1)S(1)} %copy-done.1), custom_call_target="tpu_custom_call" | custom-call | flops 1000000 | bytes 1048576 | tf_op jit(solution)/shard_map/pallas_call | solution.py:269
  15.8 4.3 %all-to-all-done.received = bf16[16,64,128]{2,1,0:T(8,128)(2,1)S(1)} async-done(((bf16[16,64,128]{2,1,0:T(8,128)(2,1)}), bf16[16,64,128]{2,1,0:T(8,128)(2,1)S(1)}, u32[]{:S(2)}, u32[]{:S(2)}) %all-to-all-start) | async-done | bytes 262176 | tf_op jit(solution)/shard_map/all_to_all | solution.py:301
  20.1 2.5 %shard_map.121 = (bf16[512,128]{1,0:T(8,128)(2,1)}, bf16[2,4,64,128]{3,2,1,0:T(8,128)(2,1)S(1)}, bf16[2,4,64,128]{3,2,1,0:T(8,128)(2,1)S(1)}) custom-call(bf16[16,64,128]{2,1,0:T(8,128)(2,1)S(1)} %all-to-all-done.received, f32[512,256]{1,0:T(8,128)S(1)} %shard_map.120.taps_values, f32[32,128]{1,0:T(8,128)S(1)} %copy-done.9, ...), custom_call_target="tpu_custom_call" | custom-call | flops 1000000 | bytes 1048576 | tf_op jit(solution)/shard_map/pallas_call | solution.py:269
  22.6 0.7 %collective-permute-start = (bf16[2,4,64,128]{3,2,1,0:T(8,128)(2,1)S(1)}, bf16[2,4,64,128]{3,2,1,0:T(8,128)(2,1)S(1)}, u32[]{:S(2)}, u32[]{:S(2)}) collective-permute-start(bf16[2,4,64,128]{3,2,1,0:T(8,128)(2,1)S(1)} %get-tuple-element.23), channel_id=1, source_target_pairs={{0,32},{16,48},{32,0},{48,16},{64,96},{80,112},{96,64},{112,80},{1... | collective-permute-start | bytes 393224 | tf_op jit(solution)/shard_map/ppermute | solution.py:342
  23.3 12.5 %all-to-all-start.1 = ((bf16[256,2,128]{2,1,0:T(2,128)(2,1)}), bf16[256,2,128]{2,1,0:T(2,128)(2,1)S(1)}, u32[]{:S(2)}, u32[]{:S(2)}) async-start(bf16[256,2,128]{2,1,0:T(2,128)(2,1)} %bitcast.2), calls=%async_computation.1 | async-start | bytes 262144 | tf_op jit(solution)/shard_map/all_to_all | solution.py:340
  35.9 0.0 collective-permute-done.came
  35.9 2.2 %collective-permute-start.1 = (bf16[2,4,64,128]{3,2,1,0:T(8,128)(2,1)S(1)}, bf16[2,4,64,128]{3,2,1,0:T(8,128)(2,1)S(1)}, u32[]{:S(2)}, u32[]{:S(2)}) collective-permute-start(bf16[2,4,64,128]{3,2,1,0:T(8,128)(2,1)S(1)} %pad_maximum_fusion), channel_id=1, source_target_pairs={{0,16},{16,0},{32,48},{48,32},{64,80},{80,64},{96,112},{112,96},{1... | collective-permute-start | bytes 393224 | tf_op jit(solution)/shard_map/ppermute | solution.py:344
  38.1 1.0 %collective-permute-done.1.crossed = bf16[2,4,64,128]{3,2,1,0:T(8,128)(2,1)S(1)} collective-permute-done((bf16[2,4,64,128]{3,2,1,0:T(8,128)(2,1)S(1)}, bf16[2,4,64,128]{3,2,1,0:T(8,128)(2,1)S(1)}, u32[]{:S(2)}, u32[]{:S(2)}) %collective-permute-start.1) | collective-permute-done | bytes 131104 | tf_op jit(solution)/shard_map/ppermute | solution.py:344
  39.1 0.1 collective-permute-start.2
  39.2 2.0 %collective-permute-start.3 = (bf16[4,64,128]{2,1,0:T(8,128)(2,1)S(1)}, bf16[4,64,128]{2,1,0:T(8,128)(2,1)S(1)}, u32[]{:S(2)}, u32[]{:S(2)}) collective-permute-start(bf16[4,64,128]{2,1,0:T(8,128)(2,1)S(1)} %get-tuple-element.26), channel_id=1, source_target_pairs={{0,128},{16,144},{32,160},{48,176},{64,192},{80,208},{96,224},{112... | collective-permute-start | bytes 196616 | tf_op jit(solution)/shard_map/ppermute | solution.py:348
  41.2 1.2 %collective-permute-start.4 = (bf16[4,64,128]{2,1,0:T(8,128)(2,1)S(1)}, bf16[4,64,128]{2,1,0:T(8,128)(2,1)S(1)}, u32[]{:S(2)}, u32[]{:S(2)}) collective-permute-start(bf16[4,64,128]{2,1,0:T(8,128)(2,1)S(1)} %get-tuple-element.27), channel_id=1, source_target_pairs={{0,192},{16,208},{32,224},{48,240},{64,0},{80,16},{96,32},{112,48}... | collective-permute-start | bytes 196616 | tf_op jit(solution)/shard_map/ppermute | solution.py:348
  42.4 3.4 %collective-permute-done.2.far1 = bf16[4,64,128]{2,1,0:T(8,128)(2,1)S(1)} collective-permute-done((bf16[4,64,128]{2,1,0:T(8,128)(2,1)S(1)}, bf16[4,64,128]{2,1,0:T(8,128)(2,1)S(1)}, u32[]{:S(2)}, u32[]{:S(2)}) %collective-permute-start.2) | collective-permute-done | bytes 65568 | tf_op jit(solution)/shard_map/ppermute | solution.py:348
  45.9 1.0 %shard_map.123 = (bf16[128,512]{1,0:T(8,128)(2,1)}, bf16[128,512]{1,0:T(8,128)(2,1)}, bf16[128,512]{1,0:T(8,128)(2,1)}, bf16[128,512]{1,0:T(8,128)(2,1)}) custom-call(bf16[4,64,128]{2,1,0:T(8,128)(2,1)S(1)} %get-tuple-element.24.far0, bf16[4,64,128]{2,1,0:T(8,128)(2,1)S(1)} %collective-permute-done.2.far1, ...), custom_call_target="tpu_custom_call" | custom-call | flops 1000000 | bytes 1048576 | tf_op jit(solution)/shard_map/pallas_call | solution.py:269
  46.9 1.7 %all-to-all-done.1 = bf16[256,2,128]{2,1,0:T(2,128)(2,1)S(1)} async-done(((bf16[256,2,128]{2,1,0:T(2,128)(2,1)}), bf16[256,2,128]{2,1,0:T(2,128)(2,1)S(1)}, u32[]{:S(2)}, u32[]{:S(2)}) %all-to-all-start.1) | async-done | bytes 131104 | tf_op jit(solution)/shard_map/all_to_all | solution.py:340
  48.5 0.9 %shard_map.124 = f32[8,8192]{1,0:T(8,128)} custom-call(bf16[512,128]{1,0:T(8,128)(2,1)S(1)} %bitcast.4), custom_call_target="tpu_custom_call" | custom-call | flops 1000000 | bytes 1048576 | tf_op jit(solution)/shard_map/pallas_call | solution.py:269
  (20 shorter events, 0.1 us)
Async XLA Ops:
  2.6 17.5 %copy-start.2 = (bf16[2,256,256]{2,1,0:T(8,128)(2,1)S(1)}, bf16[2,256,256]{2,1,0:T(8,128)(2,1)}, u32[]{:S(2)}) copy-start(bf16[2,256,256]{2,1,0:T(8,128)(2,1)} %constant.40.clone.matrix.forward) | copy-start | bytes 786436
  2.6 17.5 %copy-start.7 = (bf16[2,256,256]{2,1,0:T(8,128)(2,1)S(1)}, bf16[2,256,256]{2,1,0:T(8,128)(2,1)}, u32[]{:S(2)}) copy-start(bf16[2,256,256]{2,1,0:T(8,128)(2,1)} %constant.41.clone.backward) | copy-start | bytes 786436
  2.6 17.5 %copy-start.9 = (f32[32,128]{1,0:T(8,128)S(1)}, f32[32,128]{1,0:T(8,128)}, u32[]{:S(2)}) copy-start(f32[32,128]{1,0:T(8,128)} %constant.39.clone.twist) | copy-start | bytes 49156
  2.6 17.5 %all-to-all-start = ((bf16[16,64,128]{2,1,0:T(8,128)(2,1)}), bf16[16,64,128]{2,1,0:T(8,128)(2,1)S(1)}, u32[]{:S(2)}, u32[]{:S(2)}) async-start(bf16[16,64,128]{2,1,0:T(8,128)(2,1)} %shard_map.119), calls=%async_computation | async-start | bytes 524288 | tf_op jit(solution)/shard_map/all_to_all | solution.py:301
  11.3 1.6 %copy-start = (bf16[2048,512]{1,0:T(8,128)(2,1)S(1)}, bf16[2048,512]{1,0:T(8,128)(2,1)}, u32[]{:S(2)}) copy-start(bf16[2048,512]{1,0:T(8,128)(2,1)} %taps.1) | copy-start | bytes 6291460
  12.9 0.9 %copy-start.1 = (bf16[2,256,256]{2,1,0:T(8,128)(2,1)S(1)}, bf16[2,256,256]{2,1,0:T(8,128)(2,1)}, u32[]{:S(2)}) copy-start(bf16[2,256,256]{2,1,0:T(8,128)(2,1)} %constant.40.clone.matrix.forward) | copy-start | bytes 786436
  13.8 0.7 %copy-start.8 = (f32[32,128]{1,0:T(8,128)S(1)}, f32[32,128]{1,0:T(8,128)}, u32[]{:S(2)}) copy-start(f32[32,128]{1,0:T(8,128)} %constant.39.clone.twist) | copy-start | bytes 49156
  14.5 31.3 %copy-start.3 = (bf16[128,512]{1,0:T(8,128)(2,1)S(1)}, bf16[128,512]{1,0:T(8,128)(2,1)}, u32[]{:S(2)}) copy-start(bf16[128,512]{1,0:T(8,128)(2,1)} %out_gate.3) | copy-start | bytes 393220
  14.5 31.3 %copy-start.4 = (bf16[128,512]{1,0:T(8,128)(2,1)S(1)}, bf16[128,512]{1,0:T(8,128)(2,1)}, u32[]{:S(2)}) copy-start(bf16[128,512]{1,0:T(8,128)(2,1)} %in_gate.3) | copy-start | bytes 393220
  14.5 31.3 %copy-start.5 = (bf16[128,512]{1,0:T(8,128)(2,1)S(1)}, bf16[128,512]{1,0:T(8,128)(2,1)}, u32[]{:S(2)}) copy-start(bf16[128,512]{1,0:T(8,128)(2,1)} %values.3) | copy-start | bytes 393220
  14.5 31.3 %copy-start.6 = (bf16[128,512]{1,0:T(8,128)(2,1)S(1)}, bf16[128,512]{1,0:T(8,128)(2,1)}, u32[]{:S(2)}) copy-start(bf16[128,512]{1,0:T(8,128)(2,1)} %upstream.3) | copy-start | bytes 393220
  22.6 13.3 %collective-permute-start = (bf16[2,4,64,128]{3,2,1,0:T(8,128)(2,1)S(1)}, bf16[2,4,64,128]{3,2,1,0:T(8,128)(2,1)S(1)}, u32[]{:S(2)}, u32[]{:S(2)}) collective-permute-start(bf16[2,4,64,128]{3,2,1,0:T(8,128)(2,1)S(1)} %get-tuple-element.23), channel_id=1, source_target_pairs={{0,32},{16,48},{32,0},{48,16},{64,96},{80,112},{96,64},{112,80},{1... | collective-permute-start | bytes 393224 | tf_op jit(solution)/shard_map/ppermute | solution.py:342
  23.3 25.2 %all-to-all-start.1 = ((bf16[256,2,128]{2,1,0:T(2,128)(2,1)}), bf16[256,2,128]{2,1,0:T(2,128)(2,1)S(1)}, u32[]{:S(2)}, u32[]{:S(2)}) async-start(bf16[256,2,128]{2,1,0:T(2,128)(2,1)} %bitcast.2), calls=%async_computation.1 | async-start | bytes 262144 | tf_op jit(solution)/shard_map/all_to_all | solution.py:340
  35.9 3.2 %collective-permute-start.1 = (bf16[2,4,64,128]{3,2,1,0:T(8,128)(2,1)S(1)}, bf16[2,4,64,128]{3,2,1,0:T(8,128)(2,1)S(1)}, u32[]{:S(2)}, u32[]{:S(2)}) collective-permute-start(bf16[2,4,64,128]{3,2,1,0:T(8,128)(2,1)S(1)} %pad_maximum_fusion), channel_id=1, source_target_pairs={{0,16},{16,0},{32,48},{48,32},{64,80},{80,64},{96,112},{112,96},{1... | collective-permute-start | bytes 393224 | tf_op jit(solution)/shard_map/ppermute | solution.py:344
  39.1 6.7 %collective-permute-start.2 = (bf16[4,64,128]{2,1,0:T(8,128)(2,1)S(1)}, bf16[4,64,128]{2,1,0:T(8,128)(2,1)S(1)}, u32[]{:S(2)}, u32[]{:S(2)}) collective-permute-start(bf16[4,64,128]{2,1,0:T(8,128)(2,1)S(1)} %get-tuple-element.25), channel_id=1, source_target_pairs={{0,64},{16,80},{32,96},{48,112},{64,128},{80,144},{96,160},{112,17... | collective-permute-start | bytes 196616 | tf_op jit(solution)/shard_map/ppermute | solution.py:348
  39.2 6.6 %collective-permute-start.3 = (bf16[4,64,128]{2,1,0:T(8,128)(2,1)S(1)}, bf16[4,64,128]{2,1,0:T(8,128)(2,1)S(1)}, u32[]{:S(2)}, u32[]{:S(2)}) collective-permute-start(bf16[4,64,128]{2,1,0:T(8,128)(2,1)S(1)} %get-tuple-element.26), channel_id=1, source_target_pairs={{0,128},{16,144},{32,160},{48,176},{64,192},{80,208},{96,224},{112... | collective-permute-start | bytes 196616 | tf_op jit(solution)/shard_map/ppermute | solution.py:348
  41.2 4.6 %collective-permute-start.4 = (bf16[4,64,128]{2,1,0:T(8,128)(2,1)S(1)}, bf16[4,64,128]{2,1,0:T(8,128)(2,1)S(1)}, u32[]{:S(2)}, u32[]{:S(2)}) collective-permute-start(bf16[4,64,128]{2,1,0:T(8,128)(2,1)S(1)} %get-tuple-element.27), channel_id=1, source_target_pairs={{0,192},{16,208},{32,224},{48,240},{64,0},{80,16},{96,32},{112,48}... | collective-permute-start | bytes 196616 | tf_op jit(solution)/shard_map/ppermute | solution.py:348

commit v4 on v1

--- a/solution.py
+++ b/solution.py
@@ -11,7 +11,18 @@
 
 VMEM = 48 * 1024 * 1024
 PARTS = 2
+CTX_FIRST, CH_FIRST = 11, 9
 f32, bf16 = jnp.float32, jnp.bfloat16
+
+
+def slot(i, first, count):
+    return (i - first) % count
+
+
+def exchange(x, axis, first):
+    count = lax.axis_size(axis)
+    devices = [[(first + k) % count for k in range(count)]]
+    return lax.all_to_all(x, axis, 0, 0, tiled=True, axis_index_groups=devices)
 
 
 def leaf_angles(count, theta):
@@ -101,9 +112,10 @@
             fetch(2 * s, p).wait()
             fetch(2 * s + 1, p).wait()
             gated = (held[2 * s, p].astype(f32) * held[2 * s + 1, p].astype(f32)).astype(bf16)
-            send[first : first + part // width, s * width : (s + 1) * width, :] = gated.T.reshape(
-                part // width, width, rows
-            )
+            turned = gated.T
+            for n in range(part // width):
+                at = slot(first + n, CTX_FIRST, blocks)
+                send[at, s * width : (s + 1) * width, :] = turned[n * width : (n + 1) * width]
 
 
 def forward_part(load, twist, matrix, work, width, outer):
@@ -137,7 +149,7 @@
     blocks, width, outer = received.shape[0], received.shape[1] // 2, received.shape[2]
     for s in range(2):
         forward_part(
-            lambda i, g: received[i, s * width + 16 * g : s * width + 16 * g + 16, :].astype(f32),
+            lambda i, g: received[slot(i, CTX_FIRST, blocks), s * width + 16 * g : s * width + 16 * g + 16, :].astype(f32),
             twist, forward, work.at[s], width, outer,
         )
     step = 128
@@ -164,25 +176,24 @@
             for i, x in enumerate(interpolate(values, math.pi / 2, True)):
                 if s == 2:
                     x = x * norm_factor
-                result[i, s * width + 16 * g : s * width + 16 * g + 16, :] = x.astype(bf16)
+                result[slot(i, CTX_FIRST, blocks), s * width + 16 * g : s * width + 16 * g + 16, :] = x.astype(bf16)
+
+
+def gather_part(back, s):
+    width, blocks = back.shape[1] // 3, back.shape[0]
+    parts = [back[slot(d, CTX_FIRST, blocks), s * width : (s + 1) * width, :] for d in range(blocks)]
+    return jnp.concatenate(parts, 0).astype(f32).T
 
 
 def lags_kernel(back, lags):
-    width = back.shape[1] // 3
-    part = back[:, 2 * width :, :].astype(f32)
-    turned = part.reshape(part.shape[0] * width, part.shape[2]).T
-    lags[...] = turned.reshape(lags.shape).astype(bf16)
+    turned = gather_part(back, 2)
+    owners, rows = lags.shape[0], lags.shape[1]
+    for j in range(owners):
+        lags[slot(j, CH_FIRST, owners)] = turned[j * rows : (j + 1) * rows, :].astype(bf16)
 
 
 def gates_kernel(back, out_gate, in_gate, values, upstream, mixed_out, d_out_gate, d_in_gate, d_values):
-    width = back.shape[1] // 3
-    rows = back.shape[2]
-
-    def part(s):
-        x = back[:, s * width : (s + 1) * width, :].astype(f32)
-        return x.reshape(x.shape[0] * width, rows).T
-
-    filtered, grad_mixed = part(0), part(1)
+    filtered, grad_mixed = gather_part(back, 0), gather_part(back, 1)
     mixed_out[...] = (out_gate[...].astype(f32) * filtered).astype(bf16)
     d_out_gate[...] = (upstream[...].astype(f32) * filtered).astype(bf16)
     d_in_gate[...] = (grad_mixed * values[...].astype(f32)).astype(bf16)
@@ -190,9 +201,10 @@
 
 
 def join_kernel(arrived, grad_filter):
-    span = arrived.shape[2]
-    for j in range(arrived.shape[0]):
-        grad_filter[:, j * span : (j + 1) * span] = arrived[j].astype(f32)
+    owners, span = arrived.shape[0], arrived.shape[2]
+    for j in range(owners):
+        at = slot(j, CH_FIRST, owners)
+        grad_filter[:, j * span : (j + 1) * span] = arrived[at].astype(f32)
 
 
 def call(kernel, outs, *args, flops=1000000, vmem=VMEM, **kwargs):
@@ -225,7 +237,7 @@
             pltpu.SemaphoreType.DMA((4, PARTS)),
         ],
     )
-    received = lax.all_to_all(send, "ctx", 0, 0, tiled=True)
+    received = exchange(send, "ctx", CTX_FIRST)
 
     me = lax.axis_index("ctx")
     first = me * width
@@ -253,9 +265,9 @@
         received, taps_values, twist, forward, backward,
         scratch_shapes=[pltpu.VMEM((3, blocks * width, 2 * rows), f32)],
     )
-    back = lax.all_to_all(result, "ctx", 0, 0, tiled=True)
+    back = exchange(result, "ctx", CTX_FIRST)
     lags = call(lags_kernel, shape((owners, rows // owners, channels), bf16), back)
-    arrived = lax.all_to_all(lags, "ch", 0, 0, tiled=True)
+    arrived = exchange(lags, "ch", CH_FIRST)
     out = shape((rows, channels), bf16)
     gates = call(gates_kernel, (out,) * 4, back, out_gate, in_gate, values, upstream)
     grad_filter = call(join_kernel, shape((rows // owners, owners * channels), f32), arrived)

time: 53.8 us -> 48.3 us (0.90)
  waiting for transfers between devices: 11.8 us -> 2.76 us
  starting transfers between devices: 17 us -> 20.5 us
    all_to_all x2, waiting for transfers between devices: 11.8 us -> 2.76 us  [exchange(): return lax.all_to_all(x, axis, 0, 0, tiled=True, axis_index_groups=devices)]
    all_to_all x2, starting transfers between devices: 17 us -> 20.5 us  [exchange(): return lax.all_to_all(x, axis, 0, 0, tiled=True, axis_index_groups=devices)]
  transfers between devices with their start and end apart: 2 -> 2, of which waited for: 2 -> 1; matrix products, arithmetic and copies ran while one was open for 0% -> 0% of each run, Pallas kernels for 4% -> 5%
where the time goes in v4:
time: 48.3 us; the launch traced here: 47.9 us
  starting transfers between devices  20.5 us (42%)
  blocking collectives  13.1 us (27%)
  Pallas kernels  7.42 us (15%)
  local copies, waits for them, and re-layouts  3.3 us (7%)
  waiting for transfers between devices  2.76 us (6%)
  between operations  0.77 us (2%)
    all_to_all x2, starting transfers between devices, exchange(): return lax.all_to_all(x, axis, 0, 0, tiled=True, axis_index_groups=devices)  20.5 us
    all_to_all x1, blocking collectives, exchange(): return lax.all_to_all(x, axis, 0, 0, tiled=True, axis_index_groups=devices)  13.1 us
    pallas_call x6, Pallas kernels, call(): pl.pallas_call(kernel, out_shape=outs, compiler_params=pltpu.CompilerPara...  7.42 us
    unnamed x20, local copies, waits for them, and re-layouts  3.3 us
    all_to_all x2, waiting for transfers between devices, exchange(): return lax.all_to_all(x, axis, 0, 0, tiled=True, axis_index_groups=devices)  2.76 us
  transfers between devices with their start and end apart: 2, of which 1 were waited for; matrix products, arithmetic and copies ran while one was open for 0% of the time, Pallas kernels for 5%

profile of v4, /device:TPU:1, one launch (start us, length us, event | category | flops | bytes accessed | tf_op | source)
XLA Modules:
  0.0 47.9 jit_solution(6048109135835167145)
XLA Ops:
  0.6 2.0 %shard_map.119 = bf16[16,64,128]{2,1,0:T(8,128)(2,1)} custom-call(bf16[128,512]{1,0:T(8,128)(2,1)} %out_gate.3, bf16[128,512]{1,0:T(8,128)(2,1)} %in_gate.3, bf16[128,512]{1,0:T(8,128)(2,1)} %values.3, bf16[128,512]{1,0:T(8,128)(2,1)} %upstream.3), custom_call_target="tpu_custom_call" | custom-call | flops 1000000 | bytes 1048576 | tf_op jit(solution)/shard_map/pallas_call | solution.py:211
  2.6 0.0 copy-start.2
  2.6 0.0 copy-start.7
  2.6 0.0 copy-start.9
  2.6 10.0 %all-to-all-start = ((bf16[16,64,128]{2,1,0:T(8,128)(2,1)}), bf16[16,64,128]{2,1,0:T(8,128)(2,1)S(1)}, u32[]{:S(2)}, u32[]{:S(2)}) async-start(bf16[16,64,128]{2,1,0:T(8,128)(2,1)} %shard_map.119), calls=%async_computation | async-start | bytes 524288 | tf_op jit(solution)/shard_map/all_to_all | solution.py:25
  12.6 0.1 pad_add_fusion.index
  12.7 1.6 %copy-done = bf16[2048,512]{1,0:T(8,128)(2,1)S(1)} copy-done((bf16[2048,512]{1,0:T(8,128)(2,1)S(1)}, bf16[2048,512]{1,0:T(8,128)(2,1)}, u32[]{:S(2)}) %copy-start) | copy-done | bytes 2097176
  14.3 0.9 %copy-done.1 = bf16[2,256,256]{2,1,0:T(8,128)(2,1)S(1)} copy-done((bf16[2,256,256]{2,1,0:T(8,128)(2,1)S(1)}, bf16[2,256,256]{2,1,0:T(8,128)(2,1)}, u32[]{:S(2)}) %copy-start.1) | copy-done | bytes 262168
  15.2 0.7 %copy-done.8 = f32[32,128]{1,0:T(8,128)S(1)} copy-done((f32[32,128]{1,0:T(8,128)S(1)}, f32[32,128]{1,0:T(8,128)}, u32[]{:S(2)}) %copy-start.8) | copy-done | bytes 16408
  15.9 1.3 %shard_map.120.taps_values = f32[512,256]{1,0:T(8,128)S(1)} custom-call(s32[2]{0:T(128)S(1)} %pad_add_fusion.index, bf16[2048,512]{1,0:T(8,128)(2,1)S(1)} %copy-done, f32[32,128]{1,0:T(8,128)S(1)} %copy-done.8, bf16[2,256,256]{2,1,0:T(8,128)(2,1)S(1)} %copy-done.1), custom_call_target="tpu_custom_call" | custom-call | flops 1000000 | bytes 1048576 | tf_op jit(solution)/shard_map/pallas_call | solution.py:211
  17.2 0.0 copy-start.3
  17.2 0.0 copy-start.4
  17.2 0.0 copy-start.5
  17.2 0.0 copy-start.6
  17.3 0.0 all-to-all-done.received
  17.3 0.0 copy-done.2
  17.3 0.0 copy-done.7
  17.3 1.8 %shard_map.121 = bf16[16,96,128]{2,1,0:T(8,128)(2,1)S(1)} custom-call(bf16[16,64,128]{2,1,0:T(8,128)(2,1)S(1)} %all-to-all-done.received, f32[512,256]{1,0:T(8,128)S(1)} %shard_map.120.taps_values, f32[32,128]{1,0:T(8,128)S(1)} %copy-done.9, bf16[2,256,256]{2,1,0:T(8,128)(2,1)S(1)} %copy-done.2, bf16[2,256,256]{2,1,0:T(8,128)(2,1)S(1)} %copy-done.7), custom_call_target="tpu_custom_call" | custom-call | flops 1000000 | bytes 1048576 | tf_op jit(solution)/shard_map/pallas_call | solution.py:211
  19.1 13.1 %all_to_all.15.back = bf16[16,96,128]{2,1,0:T(8,128)(2,1)S(1)} all-to-all(bf16[16,96,128]{2,1,0:T(8,128)(2,1)S(1)} %shard_map.121), channel_id=1, replica_groups={{176,192,208,224,240,0,16,32,48,64,80,96,112,128,144,160},{177,193,209,..., dimensions={0} | all-to-all | bytes 786432 | tf_op jit(solution)/shard_map/all_to_all | solution.py:25
  32.2 0.8 %shard_map.123 = bf16[16,8,512]{2,1,0:T(8,128)(2,1)} custom-call(bf16[16,96,128]{2,1,0:T(8,128)(2,1)S(1)} %all_to_all.15.back), custom_call_target="tpu_custom_call" | custom-call | flops 1000000 | bytes 1048576 | tf_op jit(solution)/shard_map/pallas_call | solution.py:211
  32.9 10.5 %all-to-all-start.2 = ((bf16[16,8,512]{2,1,0:T(8,128)(2,1)}), bf16[16,8,512]{2,1,0:T(8,128)(2,1)S(1)}, u32[]{:S(2)}, u32[]{:S(2)}) async-start(bf16[16,8,512]{2,1,0:T(8,128)(2,1)} %shard_map.123), calls=%async_computation.2 | async-start | bytes 262144 | tf_op jit(solution)/shard_map/all_to_all | solution.py:25
  43.5 0.9 %shard_map.122 = (bf16[128,512]{1,0:T(8,128)(2,1)}, bf16[128,512]{1,0:T(8,128)(2,1)}, bf16[128,512]{1,0:T(8,128)(2,1)}, bf16[128,512]{1,0:T(8,128)(2,1)}) custom-call(bf16[16,96,128]{2,1,0:T(8,128)(2,1)S(1)} %all_to_all.15.back, bf16[128,512]{1,0:T(8,128)(2,1)S(1)} %copy-done.3, bf16[128,512]{1,0:T(8,128)(2,1)S(1)} %copy-done.4, ...), custom_call_target="tpu_custom_call" | custom-call | flops 1000000 | bytes 1048576 | tf_op jit(solution)/shard_map/pallas_call | solution.py:211
  44.4 2.8 %all-to-all-done.2.arrived = bf16[16,8,512]{2,1,0:T(8,128)(2,1)S(1)} async-done(((bf16[16,8,512]{2,1,0:T(8,128)(2,1)}), bf16[16,8,512]{2,1,0:T(8,128)(2,1)S(1)}, u32[]{:S(2)}, u32[]{:S(2)}) %all-to-all-start.2) | async-done | bytes 131104 | tf_op jit(solution)/shard_map/all_to_all | solution.py:25
  47.1 0.7 %shard_map.124 = f32[8,8192]{1,0:T(8,128)} custom-call(bf16[16,8,512]{2,1,0:T(8,128)(2,1)S(1)} %all-to-all-done.2.arrived), custom_call_target="tpu_custom_call" | custom-call | flops 1000000 | bytes 1048576 | tf_op jit(solution)/shard_map/pallas_call | solution.py:211
  (8 shorter events, 0.0 us)
Async XLA Ops:
  2.6 14.7 %copy-start.2 = (bf16[2,256,256]{2,1,0:T(8,128)(2,1)S(1)}, bf16[2,256,256]{2,1,0:T(8,128)(2,1)}, u32[]{:S(2)}) copy-start(bf16[2,256,256]{2,1,0:T(8,128)(2,1)} %constant.40.clone.matrix.forward) | copy-start | bytes 786436
  2.6 14.7 %copy-start.7 = (bf16[2,256,256]{2,1,0:T(8,128)(2,1)S(1)}, bf16[2,256,256]{2,1,0:T(8,128)(2,1)}, u32[]{:S(2)}) copy-start(bf16[2,256,256]{2,1,0:T(8,128)(2,1)} %constant.41.clone.backward) | copy-start | bytes 786436
  2.6 14.7 %copy-start.9 = (f32[32,128]{1,0:T(8,128)S(1)}, f32[32,128]{1,0:T(8,128)}, u32[]{:S(2)}) copy-start(f32[32,128]{1,0:T(8,128)} %constant.39.clone.twist) | copy-start | bytes 49156
  2.6 14.6 %all-to-all-start = ((bf16[16,64,128]{2,1,0:T(8,128)(2,1)}), bf16[16,64,128]{2,1,0:T(8,128)(2,1)S(1)}, u32[]{:S(2)}, u32[]{:S(2)}) async-start(bf16[16,64,128]{2,1,0:T(8,128)(2,1)} %shard_map.119), calls=%async_computation | async-start | bytes 524288 | tf_op jit(solution)/shard_map/all_to_all | solution.py:25
  12.7 1.6 %copy-start = (bf16[2048,512]{1,0:T(8,128)(2,1)S(1)}, bf16[2048,512]{1,0:T(8,128)(2,1)}, u32[]{:S(2)}) copy-start(bf16[2048,512]{1,0:T(8,128)(2,1)} %taps.1) | copy-start | bytes 6291460
  14.3 0.9 %copy-start.1 = (bf16[2,256,256]{2,1,0:T(8,128)(2,1)S(1)}, bf16[2,256,256]{2,1,0:T(8,128)(2,1)}, u32[]{:S(2)}) copy-start(bf16[2,256,256]{2,1,0:T(8,128)(2,1)} %constant.40.clone.matrix.forward) | copy-start | bytes 786436
  15.2 0.7 %copy-start.8 = (f32[32,128]{1,0:T(8,128)S(1)}, f32[32,128]{1,0:T(8,128)}, u32[]{:S(2)}) copy-start(f32[32,128]{1,0:T(8,128)} %constant.39.clone.twist) | copy-start | bytes 49156
  17.2 26.2 %copy-start.3 = (bf16[128,512]{1,0:T(8,128)(2,1)S(1)}, bf16[128,512]{1,0:T(8,128)(2,1)}, u32[]{:S(2)}) copy-start(bf16[128,512]{1,0:T(8,128)(2,1)} %out_gate.3) | copy-start | bytes 393220
  17.2 26.2 %copy-start.4 = (bf16[128,512]{1,0:T(8,128)(2,1)S(1)}, bf16[128,512]{1,0:T(8,128)(2,1)}, u32[]{:S(2)}) copy-start(bf16[128,512]{1,0:T(8,128)(2,1)} %in_gate.3) | copy-start | bytes 393220
  17.2 26.2 %copy-start.5 = (bf16[128,512]{1,0:T(8,128)(2,1)S(1)}, bf16[128,512]{1,0:T(8,128)(2,1)}, u32[]{:S(2)}) copy-start(bf16[128,512]{1,0:T(8,128)(2,1)} %values.3) | copy-start | bytes 393220
  17.2 26.2 %copy-start.6 = (bf16[128,512]{1,0:T(8,128)(2,1)S(1)}, bf16[128,512]{1,0:T(8,128)(2,1)}, u32[]{:S(2)}) copy-start(bf16[128,512]{1,0:T(8,128)(2,1)} %upstream.3) | copy-start | bytes 393220
  32.9 14.2 %all-to-all-start.2 = ((bf16[16,8,512]{2,1,0:T(8,128)(2,1)}), bf16[16,8,512]{2,1,0:T(8,128)(2,1)S(1)}, u32[]{:S(2)}, u32[]{:S(2)}) async-start(bf16[16,8,512]{2,1,0:T(8,128)(2,1)} %shard_map.123), calls=%async_computation.2 | async-start | bytes 262144 | tf_op jit(solution)/shard_map/all_to_all | solution.py:25

commit v5 on v4

--- a/solution.py
+++ b/solution.py
@@ -192,19 +192,19 @@
         lags[slot(j, CH_FIRST, owners)] = turned[j * rows : (j + 1) * rows, :].astype(bf16)
 
 
-def gates_kernel(back, out_gate, in_gate, values, upstream, mixed_out, d_out_gate, d_in_gate, d_values):
+def last_kernel(
+    arrived, back, out_gate, in_gate, values, upstream,
+    mixed_out, d_out_gate, d_in_gate, d_values, grad_filter,
+):
+    owners, span = arrived.shape[0], arrived.shape[2]
+    for j in range(owners):
+        at = slot(j, CH_FIRST, owners)
+        grad_filter[:, j * span : (j + 1) * span] = arrived[at].astype(f32)
     filtered, grad_mixed = gather_part(back, 0), gather_part(back, 1)
     mixed_out[...] = (out_gate[...].astype(f32) * filtered).astype(bf16)
     d_out_gate[...] = (upstream[...].astype(f32) * filtered).astype(bf16)
     d_in_gate[...] = (grad_mixed * values[...].astype(f32)).astype(bf16)
     d_values[...] = (grad_mixed * in_gate[...].astype(f32)).astype(bf16)
-
-
-def join_kernel(arrived, grad_filter):
-    owners, span = arrived.shape[0], arrived.shape[2]
-    for j in range(owners):
-        at = slot(j, CH_FIRST, owners)
-        grad_filter[:, j * span : (j + 1) * span] = arrived[at].astype(f32)
 
 
 def call(kernel, outs, *args, flops=1000000, vmem=VMEM, **kwargs):
@@ -269,9 +269,11 @@
     lags = call(lags_kernel, shape((owners, rows // owners, channels), bf16), back)
     arrived = exchange(lags, "ch", CH_FIRST)
     out = shape((rows, channels), bf16)
-    gates = call(gates_kernel, (out,) * 4, back, out_gate, in_gate, values, upstream)
-    grad_filter = call(join_kernel, shape((rows // owners, owners * channels), f32), arrived)
-    return (*gates, grad_filter)
+    return call(
+        last_kernel,
+        (out,) * 4 + (shape((rows // owners, owners * channels), f32),),
+        arrived, back, out_gate, in_gate, values, upstream,
+    )
 
 
 def solution(mesh):

time: 48.3 us -> 47.6 us (0.986)
  blocking collectives: 13.1 us -> 27 us
  starting transfers between devices: 20.5 us -> 9.97 us
  waiting for transfers between devices: 2.76 us -> 0.01 us
  Pallas kernels: 7.42 us -> 6.13 us
    all_to_all x1 -> x2, blocking collectives: 13.1 us -> 27 us  [exchange(): return lax.all_to_all(x, axis, 0, 0, tiled=True, axis_index_groups=devices)]
    all_to_all x2 -> x1, starting transfers between devices: 20.5 us -> 9.97 us  [exchange(): return lax.all_to_all(x, axis, 0, 0, tiled=True, axis_index_groups=devices)]
    all_to_all x2 -> x1, waiting for transfers between devices: 2.76 us -> 0.01 us  [exchange(): return lax.all_to_all(x, axis, 0, 0, tiled=True, axis_index_groups=devices)]
    pallas_call x6 -> x5, Pallas kernels: 7.42 us -> 6.13 us  [call(): pl.pallas_call(kernel, out_shape=outs, compiler_params=pltpu.CompilerPara...]
  transfers between devices with their start and end apart: 2 -> 1, of which waited for: 1 -> 0; matrix products, arithmetic and copies ran while one was open for 0% -> 0% of each run, Pallas kernels for 5% -> 3%
where the time goes in v5:
time: 47.6 us; the launch traced here: 47.2 us
  blocking collectives  27 us (57%)
  starting transfers between devices  9.97 us (21%)
  Pallas kernels  6.13 us (13%)
  local copies, waits for them, and re-layouts  3.3 us (7%)
  between operations  0.76 us (2%)
    all_to_all x2, blocking collectives, exchange(): return lax.all_to_all(x, axis, 0, 0, tiled=True, axis_index_groups=devices)  27 us
    all_to_all x1, starting transfers between devices, exchange(): return lax.all_to_all(x, axis, 0, 0, tiled=True, axis_index_groups=devices)  9.97 us
    pallas_call x5, Pallas kernels, call(): pl.pallas_call(kernel, out_shape=outs, compiler_params=pltpu.CompilerPara...  6.13 us
    unnamed x20, local copies, waits for them, and re-layouts  3.3 us
  transfers between devices with their start and end apart: 1, of which 0 were waited for; matrix products, arithmetic and copies ran while one was open for 0% of the time, Pallas kernels for 3%

profile of v5, /device:TPU:1, one launch (start us, length us, event | category | flops | bytes accessed | tf_op | source)
XLA Modules:
  0.0 47.2 jit_solution(13808580338648984180)
XLA Ops:
  0.6 2.0 %shard_map.119 = bf16[16,64,128]{2,1,0:T(8,128)(2,1)} custom-call(bf16[128,512]{1,0:T(8,128)(2,1)} %out_gate.3, bf16[128,512]{1,0:T(8,128)(2,1)} %in_gate.3, bf16[128,512]{1,0:T(8,128)(2,1)} %values.3, bf16[128,512]{1,0:T(8,128)(2,1)} %upstream.3), custom_call_target="tpu_custom_call" | custom-call | flops 1000000 | bytes 1048576 | tf_op jit(solution)/shard_map/pallas_call | solution.py:211
  2.6 0.0 copy-start.2
  2.6 0.0 copy-start.7
  2.6 0.0 copy-start.9
  2.6 10.0 %all-to-all-start = ((bf16[16,64,128]{2,1,0:T(8,128)(2,1)}), bf16[16,64,128]{2,1,0:T(8,128)(2,1)S(1)}, u32[]{:S(2)}, u32[]{:S(2)}) async-start(bf16[16,64,128]{2,1,0:T(8,128)(2,1)} %shard_map.119), calls=%async_computation | async-start | bytes 524288 | tf_op jit(solution)/shard_map/all_to_all | solution.py:25
  12.6 0.1 pad_add_fusion.index
  12.7 1.6 %copy-done = bf16[2048,512]{1,0:T(8,128)(2,1)S(1)} copy-done((bf16[2048,512]{1,0:T(8,128)(2,1)S(1)}, bf16[2048,512]{1,0:T(8,128)(2,1)}, u32[]{:S(2)}) %copy-start) | copy-done | bytes 2097176
  14.3 0.9 %copy-done.1 = bf16[2,256,256]{2,1,0:T(8,128)(2,1)S(1)} copy-done((bf16[2,256,256]{2,1,0:T(8,128)(2,1)S(1)}, bf16[2,256,256]{2,1,0:T(8,128)(2,1)}, u32[]{:S(2)}) %copy-start.1) | copy-done | bytes 262168
  15.2 0.7 %copy-done.8 = f32[32,128]{1,0:T(8,128)S(1)} copy-done((f32[32,128]{1,0:T(8,128)S(1)}, f32[32,128]{1,0:T(8,128)}, u32[]{:S(2)}) %copy-start.8) | copy-done | bytes 16408
  15.9 1.3 %shard_map.120.taps_values = f32[512,256]{1,0:T(8,128)S(1)} custom-call(s32[2]{0:T(128)S(1)} %pad_add_fusion.index, bf16[2048,512]{1,0:T(8,128)(2,1)S(1)} %copy-done, f32[32,128]{1,0:T(8,128)S(1)} %copy-done.8, bf16[2,256,256]{2,1,0:T(8,128)(2,1)S(1)} %copy-done.1), custom_call_target="tpu_custom_call" | custom-call | flops 1000000 | bytes 1048576 | tf_op jit(solution)/shard_map/pallas_call | solution.py:211
  17.2 0.0 copy-start.3
  17.2 0.0 copy-start.4
  17.2 0.0 copy-start.5
  17.2 0.0 copy-start.6
  17.3 0.0 all-to-all-done.received
  17.3 0.0 copy-done.2
  17.3 0.0 copy-done.7
  17.3 0.0 copy-done.9
  17.3 1.8 %shard_map.121 = bf16[16,96,128]{2,1,0:T(8,128)(2,1)S(1)} custom-call(bf16[16,64,128]{2,1,0:T(8,128)(2,1)S(1)} %all-to-all-done.received, f32[512,256]{1,0:T(8,128)S(1)} %shard_map.120.taps_values, f32[32,128]{1,0:T(8,128)S(1)} %copy-done.9, bf16[2,256,256]{2,1,0:T(8,128)(2,1)S(1)} %copy-done.2, bf16[2,256,256]{2,1,0:T(8,128)(2,1)S(1)} %copy-done.7), custom_call_target="tpu_custom_call" | custom-call | flops 1000000 | bytes 1048576 | tf_op jit(solution)/shard_map/pallas_call | solution.py:211
  19.1 13.1 %all_to_all.15.back = bf16[16,96,128]{2,1,0:T(8,128)(2,1)S(1)} all-to-all(bf16[16,96,128]{2,1,0:T(8,128)(2,1)S(1)} %shard_map.121), channel_id=1, replica_groups={{176,192,208,224,240,0,16,32,48,64,80,96,112,128,144,160},{177,193,209,..., dimensions={0} | all-to-all | bytes 786432 | tf_op jit(solution)/shard_map/all_to_all | solution.py:25
  32.2 0.1 shard_map.122
  32.3 13.9 %all_to_all.16.arrived = bf16[16,8,512]{2,1,0:T(8,128)(2,1)S(1)} all-to-all(bf16[16,8,512]{2,1,0:T(8,128)(2,1)S(1)} %shard_map.122), channel_id=1, replica_groups={{9,10,11,12,13,14,15,0,1,2,3,4,5,6,7,8},{25,26,27,28,29,30,31,16,17,18,..., dimensions={0} | all-to-all | bytes 262144 | tf_op jit(solution)/shard_map/all_to_all | solution.py:25
  46.2 0.0 copy-done.3
  46.2 1.0 %shard_map.123 = (bf16[128,512]{1,0:T(8,128)(2,1)}, bf16[128,512]{1,0:T(8,128)(2,1)}, bf16[128,512]{1,0:T(8,128)(2,1)}, bf16[128,512]{1,0:T(8,128)(2,1)}, f32[8,8192]{1,0:T(8,128)}) custom-call(bf16[16,8,512]{2,1,0:T(8,128)(2,1)S(1)} %all_to_all.16.arrived, bf16[16,96,128]{2,1,0:T(8,128)(2,1)S(1)} %all_to_all.15.back, bf16[128,512]{1,0:T(8,128)(2,1)S(1)} %copy-done.3, ...), custom_call_target="tpu_custom_call" | custom-call | flops 1000000 | bytes 1048576 | tf_op jit(solution)/shard_map/pallas_call | solution.py:211
  (6 shorter events, 0.0 us)
Async XLA Ops:
  2.6 14.7 %copy-start.2 = (bf16[2,256,256]{2,1,0:T(8,128)(2,1)S(1)}, bf16[2,256,256]{2,1,0:T(8,128)(2,1)}, u32[]{:S(2)}) copy-start(bf16[2,256,256]{2,1,0:T(8,128)(2,1)} %constant.40.clone.matrix.forward) | copy-start | bytes 786436
  2.6 14.7 %copy-start.7 = (bf16[2,256,256]{2,1,0:T(8,128)(2,1)S(1)}, bf16[2,256,256]{2,1,0:T(8,128)(2,1)}, u32[]{:S(2)}) copy-start(bf16[2,256,256]{2,1,0:T(8,128)(2,1)} %constant.41.clone.backward) | copy-start | bytes 786436
  2.6 14.7 %copy-start.9 = (f32[32,128]{1,0:T(8,128)S(1)}, f32[32,128]{1,0:T(8,128)}, u32[]{:S(2)}) copy-start(f32[32,128]{1,0:T(8,128)} %constant.39.clone.twist) | copy-start | bytes 49156
  2.6 14.6 %all-to-all-start = ((bf16[16,64,128]{2,1,0:T(8,128)(2,1)}), bf16[16,64,128]{2,1,0:T(8,128)(2,1)S(1)}, u32[]{:S(2)}, u32[]{:S(2)}) async-start(bf16[16,64,128]{2,1,0:T(8,128)(2,1)} %shard_map.119), calls=%async_computation | async-start | bytes 524288 | tf_op jit(solution)/shard_map/all_to_all | solution.py:25
  12.7 1.6 %copy-start = (bf16[2048,512]{1,0:T(8,128)(2,1)S(1)}, bf16[2048,512]{1,0:T(8,128)(2,1)}, u32[]{:S(2)}) copy-start(bf16[2048,512]{1,0:T(8,128)(2,1)} %taps.1) | copy-start | bytes 6291460
  14.3 0.9 %copy-start.1 = (bf16[2,256,256]{2,1,0:T(8,128)(2,1)S(1)}, bf16[2,256,256]{2,1,0:T(8,128)(2,1)}, u32[]{:S(2)}) copy-start(bf16[2,256,256]{2,1,0:T(8,128)(2,1)} %constant.40.clone.matrix.forward) | copy-start | bytes 786436
  15.2 0.7 %copy-start.8 = (f32[32,128]{1,0:T(8,128)S(1)}, f32[32,128]{1,0:T(8,128)}, u32[]{:S(2)}) copy-start(f32[32,128]{1,0:T(8,128)} %constant.39.clone.twist) | copy-start | bytes 49156
  17.2 29.0 %copy-start.3 = (bf16[128,512]{1,0:T(8,128)(2,1)S(1)}, bf16[128,512]{1,0:T(8,128)(2,1)}, u32[]{:S(2)}) copy-start(bf16[128,512]{1,0:T(8,128)(2,1)} %out_gate.3) | copy-start | bytes 393220
  17.2 29.0 %copy-start.4 = (bf16[128,512]{1,0:T(8,128)(2,1)S(1)}, bf16[128,512]{1,0:T(8,128)(2,1)}, u32[]{:S(2)}) copy-start(bf16[128,512]{1,0:T(8,128)(2,1)} %in_gate.3) | copy-start | bytes 393220
  17.2 29.0 %copy-start.5 = (bf16[128,512]{1,0:T(8,128)(2,1)S(1)}, bf16[128,512]{1,0:T(8,128)(2,1)}, u32[]{:S(2)}) copy-start(bf16[128,512]{1,0:T(8,128)(2,1)} %values.3) | copy-start | bytes 393220
  17.2 29.0 %copy-start.6 = (bf16[128,512]{1,0:T(8,128)(2,1)S(1)}, bf16[128,512]{1,0:T(8,128)(2,1)}, u32[]{:S(2)}) copy-start(bf16[128,512]{1,0:T(8,128)(2,1)} %upstream.3) | copy-start | bytes 393220

commit v6 on v5

--- a/solution.py
+++ b/solution.py
@@ -11,7 +11,7 @@
 
 VMEM = 48 * 1024 * 1024
 PARTS = 2
-CTX_FIRST, CH_FIRST = 11, 9
+IN_FIRST, CTX_FIRST, CH_FIRST = 15, 11, 9
 f32, bf16 = jnp.float32, jnp.bfloat16
 
 
@@ -114,7 +114,7 @@
             gated = (held[2 * s, p].astype(f32) * held[2 * s + 1, p].astype(f32)).astype(bf16)
             turned = gated.T
             for n in range(part // width):
-                at = slot(first + n, CTX_FIRST, blocks)
+                at = slot(first + n, IN_FIRST, blocks)
                 send[at, s * width : (s + 1) * width, :] = turned[n * width : (n + 1) * width]
 
 
@@ -149,7 +149,7 @@
     blocks, width, outer = received.shape[0], received.shape[1] // 2, received.shape[2]
     for s in range(2):
         forward_part(
-            lambda i, g: received[slot(i, CTX_FIRST, blocks), s * width + 16 * g : s * width + 16 * g + 16, :].astype(f32),
+            lambda i, g: received[slot(i, IN_FIRST, blocks), s * width + 16 * g : s * width + 16 * g + 16, :].astype(f32),
             twist, forward, work.at[s], width, outer,
         )
     step = 128
@@ -237,7 +237,7 @@
             pltpu.SemaphoreType.DMA((4, PARTS)),
         ],
     )
-    received = exchange(send, "ctx", CTX_FIRST)
+    received = exchange(send, "ctx", IN_FIRST)
 
     me = lax.axis_index("ctx")
     first = me * width

time: 47.6 us -> 47.3 us (level)
  transfers between devices with their start and end apart: 1 -> 1, of which waited for: 0 -> 1; matrix products, arithmetic and copies ran while one was open for 0% -> 0% of each run, Pallas kernels for 3% -> 3%
where the time goes in v6:
time: 47.3 us; the launch traced here: 46.9 us
  blocking collectives  26.7 us (56%)
  starting transfers between devices  9.67 us (20%)
  Pallas kernels  6.13 us (13%)
  local copies, waits for them, and re-layouts  3.3 us (7%)
  between operations  0.74 us (2%)
    all_to_all x2, blocking collectives, exchange(): return lax.all_to_all(x, axis, 0, 0, tiled=True, axis_index_groups=devices)  26.7 us
    all_to_all x1, starting transfers between devices, exchange(): return lax.all_to_all(x, axis, 0, 0, tiled=True, axis_index_groups=devices)  9.67 us
    pallas_call x5, Pallas kernels, call(): pl.pallas_call(kernel, out_shape=outs, compiler_params=pltpu.CompilerPara...  6.13 us
    unnamed x20, local copies, waits for them, and re-layouts  3.3 us
  transfers between devices with their start and end apart: 1, of which 1 were waited for; matrix products, arithmetic and copies ran while one was open for 0% of the time, Pallas kernels for 3%

profile of v6, /device:TPU:1, one launch (start us, length us, event | category | flops | bytes accessed | tf_op | source)
XLA Modules:
  0.0 46.9 jit_solution(10304124837970429864)
XLA Ops:
  0.6 2.0 %shard_map.119 = bf16[16,64,128]{2,1,0:T(8,128)(2,1)} custom-call(bf16[128,512]{1,0:T(8,128)(2,1)} %out_gate.3, bf16[128,512]{1,0:T(8,128)(2,1)} %in_gate.3, bf16[128,512]{1,0:T(8,128)(2,1)} %values.3, bf16[128,512]{1,0:T(8,128)(2,1)} %upstream.3), custom_call_target="tpu_custom_call" | custom-call | flops 1000000 | bytes 1048576 | tf_op jit(solution)/shard_map/pallas_call | solution.py:211
  2.6 0.0 copy-start.2
  2.6 0.0 copy-start.7
  2.6 0.0 copy-start.9
  2.6 9.7 %all-to-all-start = ((bf16[16,64,128]{2,1,0:T(8,128)(2,1)}), bf16[16,64,128]{2,1,0:T(8,128)(2,1)S(1)}, u32[]{:S(2)}, u32[]{:S(2)}) async-start(bf16[16,64,128]{2,1,0:T(8,128)(2,1)} %shard_map.119), calls=%async_computation | async-start | bytes 524288 | tf_op jit(solution)/shard_map/all_to_all | solution.py:25
  12.3 0.1 pad_add_fusion.index
  12.4 1.6 %copy-done = bf16[2048,512]{1,0:T(8,128)(2,1)S(1)} copy-done((bf16[2048,512]{1,0:T(8,128)(2,1)S(1)}, bf16[2048,512]{1,0:T(8,128)(2,1)}, u32[]{:S(2)}) %copy-start) | copy-done | bytes 2097176
  14.0 0.9 %copy-done.1 = bf16[2,256,256]{2,1,0:T(8,128)(2,1)S(1)} copy-done((bf16[2,256,256]{2,1,0:T(8,128)(2,1)S(1)}, bf16[2,256,256]{2,1,0:T(8,128)(2,1)}, u32[]{:S(2)}) %copy-start.1) | copy-done | bytes 262168
  14.9 0.7 %copy-done.8 = f32[32,128]{1,0:T(8,128)S(1)} copy-done((f32[32,128]{1,0:T(8,128)S(1)}, f32[32,128]{1,0:T(8,128)}, u32[]{:S(2)}) %copy-start.8) | copy-done | bytes 16408
  15.6 1.3 %shard_map.120.taps_values = f32[512,256]{1,0:T(8,128)S(1)} custom-call(s32[2]{0:T(128)S(1)} %pad_add_fusion.index, bf16[2048,512]{1,0:T(8,128)(2,1)S(1)} %copy-done, f32[32,128]{1,0:T(8,128)S(1)} %copy-done.8, bf16[2,256,256]{2,1,0:T(8,128)(2,1)S(1)} %copy-done.1), custom_call_target="tpu_custom_call" | custom-call | flops 1000000 | bytes 1048576 | tf_op jit(solution)/shard_map/pallas_call | solution.py:211
  16.9 0.0 copy-start.3
  16.9 0.0 copy-start.4
  16.9 0.0 copy-start.5
  16.9 0.0 copy-start.6
  17.0 0.3 all-to-all-done.received
  17.3 0.0 copy-done.2
  17.3 0.0 copy-done.9
  17.3 1.8 %shard_map.121 = bf16[16,96,128]{2,1,0:T(8,128)(2,1)S(1)} custom-call(bf16[16,64,128]{2,1,0:T(8,128)(2,1)S(1)} %all-to-all-done.received, f32[512,256]{1,0:T(8,128)S(1)} %shard_map.120.taps_values, f32[32,128]{1,0:T(8,128)S(1)} %copy-done.9, bf16[2,256,256]{2,1,0:T(8,128)(2,1)S(1)} %copy-done.2, bf16[2,256,256]{2,1,0:T(8,128)(2,1)S(1)} %copy-done.7), custom_call_target="tpu_custom_call" | custom-call | flops 1000000 | bytes 1048576 | tf_op jit(solution)/shard_map/pallas_call | solution.py:211
  19.1 12.8 %all_to_all.15.back = bf16[16,96,128]{2,1,0:T(8,128)(2,1)S(1)} all-to-all(bf16[16,96,128]{2,1,0:T(8,128)(2,1)S(1)} %shard_map.121), channel_id=1, replica_groups={{176,192,208,224,240,0,16,32,48,64,80,96,112,128,144,160},{177,193,209,..., dimensions={0} | all-to-all | bytes 786432 | tf_op jit(solution)/shard_map/all_to_all | solution.py:25
  31.9 0.1 shard_map.122
  32.0 13.9 %all_to_all.16.arrived = bf16[16,8,512]{2,1,0:T(8,128)(2,1)S(1)} all-to-all(bf16[16,8,512]{2,1,0:T(8,128)(2,1)S(1)} %shard_map.122), channel_id=1, replica_groups={{9,10,11,12,13,14,15,0,1,2,3,4,5,6,7,8},{25,26,27,28,29,30,31,16,17,18,..., dimensions={0} | all-to-all | bytes 262144 | tf_op jit(solution)/shard_map/all_to_all | solution.py:25
  45.9 0.0 copy-done.5
  45.9 0.0 copy-done.6
  45.9 1.0 %shard_map.123 = (bf16[128,512]{1,0:T(8,128)(2,1)}, bf16[128,512]{1,0:T(8,128)(2,1)}, bf16[128,512]{1,0:T(8,128)(2,1)}, bf16[128,512]{1,0:T(8,128)(2,1)}, f32[8,8192]{1,0:T(8,128)}) custom-call(bf16[16,8,512]{2,1,0:T(8,128)(2,1)S(1)} %all_to_all.16.arrived, bf16[16,96,128]{2,1,0:T(8,128)(2,1)S(1)} %all_to_all.15.back, bf16[128,512]{1,0:T(8,128)(2,1)S(1)} %copy-done.3, ...), custom_call_target="tpu_custom_call" | custom-call | flops 1000000 | bytes 1048576 | tf_op jit(solution)/shard_map/pallas_call | solution.py:211
  (6 shorter events, 0.0 us)
Async XLA Ops:
  2.6 14.7 %copy-start.2 = (bf16[2,256,256]{2,1,0:T(8,128)(2,1)S(1)}, bf16[2,256,256]{2,1,0:T(8,128)(2,1)}, u32[]{:S(2)}) copy-start(bf16[2,256,256]{2,1,0:T(8,128)(2,1)} %constant.40.clone.matrix.forward) | copy-start | bytes 786436
  2.6 14.7 %copy-start.7 = (bf16[2,256,256]{2,1,0:T(8,128)(2,1)S(1)}, bf16[2,256,256]{2,1,0:T(8,128)(2,1)}, u32[]{:S(2)}) copy-start(bf16[2,256,256]{2,1,0:T(8,128)(2,1)} %constant.41.clone.backward) | copy-start | bytes 786436
  2.6 14.7 %copy-start.9 = (f32[32,128]{1,0:T(8,128)S(1)}, f32[32,128]{1,0:T(8,128)}, u32[]{:S(2)}) copy-start(f32[32,128]{1,0:T(8,128)} %constant.39.clone.twist) | copy-start | bytes 49156
  2.6 14.6 %all-to-all-start = ((bf16[16,64,128]{2,1,0:T(8,128)(2,1)}), bf16[16,64,128]{2,1,0:T(8,128)(2,1)S(1)}, u32[]{:S(2)}, u32[]{:S(2)}) async-start(bf16[16,64,128]{2,1,0:T(8,128)(2,1)} %shard_map.119), calls=%async_computation | async-start | bytes 524288 | tf_op jit(solution)/shard_map/all_to_all | solution.py:25
  12.4 1.6 %copy-start = (bf16[2048,512]{1,0:T(8,128)(2,1)S(1)}, bf16[2048,512]{1,0:T(8,128)(2,1)}, u32[]{:S(2)}) copy-start(bf16[2048,512]{1,0:T(8,128)(2,1)} %taps.1) | copy-start | bytes 6291460
  14.0 0.9 %copy-start.1 = (bf16[2,256,256]{2,1,0:T(8,128)(2,1)S(1)}, bf16[2,256,256]{2,1,0:T(8,128)(2,1)}, u32[]{:S(2)}) copy-start(bf16[2,256,256]{2,1,0:T(8,128)(2,1)} %constant.40.clone.matrix.forward) | copy-start | bytes 786436
  14.9 0.7 %copy-start.8 = (f32[32,128]{1,0:T(8,128)S(1)}, f32[32,128]{1,0:T(8,128)}, u32[]{:S(2)}) copy-start(f32[32,128]{1,0:T(8,128)} %constant.39.clone.twist) | copy-start | bytes 49156
  16.9 29.0 %copy-start.3 = (bf16[128,512]{1,0:T(8,128)(2,1)S(1)}, bf16[128,512]{1,0:T(8,128)(2,1)}, u32[]{:S(2)}) copy-start(bf16[128,512]{1,0:T(8,128)(2,1)} %out_gate.3) | copy-start | bytes 393220
  16.9 29.0 %copy-start.4 = (bf16[128,512]{1,0:T(8,128)(2,1)S(1)}, bf16[128,512]{1,0:T(8,128)(2,1)}, u32[]{:S(2)}) copy-start(bf16[128,512]{1,0:T(8,128)(2,1)} %in_gate.3) | copy-start | bytes 393220
  16.9 29.0 %copy-start.5 = (bf16[128,512]{1,0:T(8,128)(2,1)S(1)}, bf16[128,512]{1,0:T(8,128)(2,1)}, u32[]{:S(2)}) copy-start(bf16[128,512]{1,0:T(8,128)(2,1)} %values.3) | copy-start | bytes 393220
  16.9 29.0 %copy-start.6 = (bf16[128,512]{1,0:T(8,128)(2,1)S(1)}, bf16[128,512]{1,0:T(8,128)(2,1)}, u32[]{:S(2)}) copy-start(bf16[128,512]{1,0:T(8,128)(2,1)} %upstream.3) | copy-start | bytes 393220

commit v7 on v6

--- a/solution.py
+++ b/solution.py
@@ -83,14 +83,28 @@
         rest = (m - top.astype(np.float64)).astype(np.float32).astype(ml_dtypes.bfloat16)
         return np.stack([top, rest])
 
-    return twist, split(forward), split(backward)
+    rest, parts = np.concatenate([twist[:blocks], twist[blocks:]], 1), []
+    for _ in range(3):
+        parts.append(rest.astype(ml_dtypes.bfloat16))
+        rest = rest - parts[-1].astype(np.float32)
+    table = np.concatenate([*split(forward), *parts], 0)
+    return twist, split(forward), split(backward), table
+
+
+def read_table(table, twist):
+    blocks, outer = twist.shape[0] // 2, twist.shape[1]
+    rest = table[4 * outer :, :].astype(f32)
+    total = (rest[2 * blocks :] + rest[blocks : 2 * blocks]) + rest[:blocks]
+    twist[:blocks, :] = total[:, :outer]
+    twist[blocks:, :] = total[:, outer:]
+    return table.at[: 2 * outer], table.at[2 * outer : 4 * outer]
 
 
 def accurate_dot(x, m_ref):
     top = x.astype(bf16)
     rest = (x - top.astype(f32)).astype(bf16)
     dot = lambda a, b: jnp.dot(a, b, preferred_element_type=f32)
-    return dot(top, m_ref[0]) + (dot(rest, m_ref[0]) + dot(top, m_ref[1]))
+    return dot(top, m_ref[0][...]) + (dot(rest, m_ref[0][...]) + dot(top, m_ref[1][...]))
 
 
 def send_kernel(out_gate, in_gate, values, upstream, send, held, arrived):
@@ -132,7 +146,8 @@
         work[r : r + step, :] = accurate_dot(work[r : r + step, :], matrix)
 
 
-def taps_kernel(index, taps, twist, matrix, spectrum, turned):
+def taps_kernel(index, taps, table, spectrum, turned, twist):
+    matrix = read_table(table, twist)
     blocks, outer = twist.shape[0] // 2, twist.shape[1]
     width = spectrum.shape[0] // blocks
     for i in range(blocks):
@@ -224,7 +239,7 @@
     owners = lax.axis_size("ch")
     width = channels // blocks
     shape = jax.ShapeDtypeStruct
-    twist, forward, backward = (jnp.asarray(t) for t in tables(blocks, rows))
+    twist, forward, backward, table = (jnp.asarray(t) for t in tables(blocks, rows))
 
     send = call(
         send_kernel,
@@ -246,17 +261,19 @@
     taps_values = call(
         taps_kernel,
         shape((blocks * width, 2 * rows), f32),
-        index, filter_taps, twist, forward,
+        index, filter_taps, table,
         grid_spec=pltpu.PrefetchScalarGridSpec(
             num_scalar_prefetch=1,
             grid=(1,),
             in_specs=[
                 pl.BlockSpec((seq_len, 128), lambda g, index: (0, index[0])),
-                whole(twist.shape),
-                whole(forward.shape),
+                whole(table.shape),
             ],
             out_specs=whole((blocks * width, 2 * rows)),
-            scratch_shapes=[pltpu.VMEM((blocks, 128, rows), f32)],
+            scratch_shapes=[
+                pltpu.VMEM((blocks, 128, rows), f32),
+                pltpu.VMEM((2 * blocks, rows), f32),
+            ],
         ),
     )
     result = call(

time: 47.3 us -> 47.3 us (level)
  local copies, waits for them, and re-layouts: 3.3 us -> 2.59 us
  waiting for transfers between devices: 0.31 us -> 1.01 us
    unnamed x20 -> x18, local copies, waits for them, and re-layouts: 3.3 us -> 2.59 us
    all_to_all x1, waiting for transfers between devices: 0.31 us -> 1.01 us  [exchange(): return lax.all_to_all(x, axis, 0, 0, tiled=True, axis_index_groups=devices)]
where the time goes in v7:
time: 47.3 us; the launch traced here: 46.9 us
  blocking collectives  26.7 us (56%)
  starting transfers between devices  9.67 us (20%)
  Pallas kernels  6.14 us (13%)
  local copies, waits for them, and re-layouts  2.59 us (5%)
  waiting for transfers between devices  1.01 us (2%)
  between operations  0.74 us (2%)
    all_to_all x2, blocking collectives, exchange(): return lax.all_to_all(x, axis, 0, 0, tiled=True, axis_index_groups=devices)  26.7 us
    all_to_all x1, starting transfers between devices, exchange(): return lax.all_to_all(x, axis, 0, 0, tiled=True, axis_index_groups=devices)  9.67 us
    pallas_call x5, Pallas kernels, call(): pl.pallas_call(kernel, out_shape=outs, compiler_params=pltpu.CompilerPara...  6.14 us
    unnamed x18, local copies, waits for them, and re-layouts  2.59 us
    all_to_all x1, waiting for transfers between devices, exchange(): return lax.all_to_all(x, axis, 0, 0, tiled=True, axis_index_groups=devices)  1.01 us
  transfers between devices with their start and end apart: 1, of which 1 were waited for; matrix products, arithmetic and copies ran while one was open for 0% of the time, Pallas kernels for 3%

profile of v7, /device:TPU:1, one launch (start us, length us, event | category | flops | bytes accessed | tf_op | source)
XLA Modules:
  0.0 46.9 jit_solution(15860829665229454191)
XLA Ops:
  0.6 2.0 %shard_map.128 = bf16[16,64,128]{2,1,0:T(8,128)(2,1)} custom-call(bf16[128,512]{1,0:T(8,128)(2,1)} %out_gate.3, bf16[128,512]{1,0:T(8,128)(2,1)} %in_gate.3, bf16[128,512]{1,0:T(8,128)(2,1)} %values.3, bf16[128,512]{1,0:T(8,128)(2,1)} %upstream.3), custom_call_target="tpu_custom_call" | custom-call | flops 1000000 | bytes 1048576 | tf_op jit(solution)/shard_map/pallas_call | solution.py:226
  2.6 0.0 copy-start.6
  2.6 0.0 copy-start.7
  2.6 0.0 copy-start.8
  2.6 9.7 %all-to-all-start = ((bf16[16,64,128]{2,1,0:T(8,128)(2,1)}), bf16[16,64,128]{2,1,0:T(8,128)(2,1)S(1)}, u32[]{:S(2)}, u32[]{:S(2)}) async-start(bf16[16,64,128]{2,1,0:T(8,128)(2,1)} %shard_map.128), calls=%async_computation | async-start | bytes 524288 | tf_op jit(solution)/shard_map/all_to_all | solution.py:25
  12.3 0.1 pad_add_fusion.index
  12.4 1.6 %copy-done = bf16[2048,512]{1,0:T(8,128)(2,1)S(1)} copy-done((bf16[2048,512]{1,0:T(8,128)(2,1)S(1)}, bf16[2048,512]{1,0:T(8,128)(2,1)}, u32[]{:S(2)}) %copy-start) | copy-done | bytes 2097176
  14.0 1.0 %copy-done.5 = bf16[560,256]{1,0:T(8,128)(2,1)S(1)} copy-done((bf16[560,256]{1,0:T(8,128)(2,1)S(1)}, bf16[560,256]{1,0:T(8,128)(2,1)}, u32[]{:S(2)}) %copy-start.5) | copy-done | bytes 286744
  14.9 1.3 %shard_map.129.taps_values = f32[512,256]{1,0:T(8,128)S(1)} custom-call(s32[2]{0:T(128)S(1)} %pad_add_fusion.index, bf16[2048,512]{1,0:T(8,128)(2,1)S(1)} %copy-done, bf16[560,256]{1,0:T(8,128)(2,1)S(1)} %copy-done.5), custom_call_target="tpu_custom_call" | custom-call | flops 1000000 | bytes 1048576 | tf_op jit(solution)/shard_map/pallas_call | solution.py:226
  16.2 0.0 copy-start.1
  16.2 0.0 copy-start.2
  16.2 0.0 copy-start.3
  16.2 0.0 copy-start.4
  16.3 1.0 %all-to-all-done.received = bf16[16,64,128]{2,1,0:T(8,128)(2,1)S(1)} async-done(((bf16[16,64,128]{2,1,0:T(8,128)(2,1)}), bf16[16,64,128]{2,1,0:T(8,128)(2,1)S(1)}, u32[]{:S(2)}, u32[]{:S(2)}) %all-to-all-start) | async-done | bytes 262176 | tf_op jit(solution)/shard_map/all_to_all | solution.py:25
  17.3 0.0 copy-done.6
  17.3 0.0 copy-done.7
  17.3 0.0 copy-done.8
  17.3 1.8 %shard_map.130 = bf16[16,96,128]{2,1,0:T(8,128)(2,1)S(1)} custom-call(bf16[16,64,128]{2,1,0:T(8,128)(2,1)S(1)} %all-to-all-done.received, f32[512,256]{1,0:T(8,128)S(1)} %shard_map.129.taps_values, f32[32,128]{1,0:T(8,128)S(1)} %copy-done.8, bf16[2,256,256]{2,1,0:T(8,128)(2,1)S(1)} %copy-done.7, bf16[2,256,256]{2,1,0:T(8,128)(2,1)S(1)} %copy-done.6), custom_call_target="tpu_custom_call" | custom-call | flops 1000000 | bytes 1048576 | tf_op jit(solution)/shard_map/pallas_call | solution.py:226
  19.1 12.8 %all_to_all.15.back = bf16[16,96,128]{2,1,0:T(8,128)(2,1)S(1)} all-to-all(bf16[16,96,128]{2,1,0:T(8,128)(2,1)S(1)} %shard_map.130), channel_id=1, replica_groups={{176,192,208,224,240,0,16,32,48,64,80,96,112,128,144,160},{177,193,209,..., dimensions={0} | all-to-all | bytes 786432 | tf_op jit(solution)/shard_map/all_to_all | solution.py:25
  31.9 0.1 shard_map.131
  32.0 13.9 %all_to_all.16.arrived = bf16[16,8,512]{2,1,0:T(8,128)(2,1)S(1)} all-to-all(bf16[16,8,512]{2,1,0:T(8,128)(2,1)S(1)} %shard_map.131), channel_id=1, replica_groups={{9,10,11,12,13,14,15,0,1,2,3,4,5,6,7,8},{25,26,27,28,29,30,31,16,17,18,..., dimensions={0} | all-to-all | bytes 262144 | tf_op jit(solution)/shard_map/all_to_all | solution.py:25
  45.9 0.0 copy-done.3
  45.9 0.0 copy-done.4
  45.9 1.0 %shard_map.132 = (bf16[128,512]{1,0:T(8,128)(2,1)}, bf16[128,512]{1,0:T(8,128)(2,1)}, bf16[128,512]{1,0:T(8,128)(2,1)}, bf16[128,512]{1,0:T(8,128)(2,1)}, f32[8,8192]{1,0:T(8,128)}) custom-call(bf16[16,8,512]{2,1,0:T(8,128)(2,1)S(1)} %all_to_all.16.arrived, bf16[16,96,128]{2,1,0:T(8,128)(2,1)S(1)} %all_to_all.15.back, bf16[128,512]{1,0:T(8,128)(2,1)S(1)} %copy-done.1, ...), custom_call_target="tpu_custom_call" | custom-call | flops 1000000 | bytes 1048576 | tf_op jit(solution)/shard_map/pallas_call | solution.py:226
  (4 shorter events, 0.0 us)
Async XLA Ops:
  2.6 14.7 %copy-start.6 = (bf16[2,256,256]{2,1,0:T(8,128)(2,1)S(1)}, bf16[2,256,256]{2,1,0:T(8,128)(2,1)}, u32[]{:S(2)}) copy-start(bf16[2,256,256]{2,1,0:T(8,128)(2,1)} %constant.43.clone.backward) | copy-start | bytes 786436
  2.6 14.7 %copy-start.7 = (bf16[2,256,256]{2,1,0:T(8,128)(2,1)S(1)}, bf16[2,256,256]{2,1,0:T(8,128)(2,1)}, u32[]{:S(2)}) copy-start(bf16[2,256,256]{2,1,0:T(8,128)(2,1)} %constant.42.clone.forward) | copy-start | bytes 786436
  2.6 14.7 %copy-start.8 = (f32[32,128]{1,0:T(8,128)S(1)}, f32[32,128]{1,0:T(8,128)}, u32[]{:S(2)}) copy-start(f32[32,128]{1,0:T(8,128)} %constant.41.clone.twist) | copy-start | bytes 49156
  2.6 14.6 %all-to-all-start = ((bf16[16,64,128]{2,1,0:T(8,128)(2,1)}), bf16[16,64,128]{2,1,0:T(8,128)(2,1)S(1)}, u32[]{:S(2)}, u32[]{:S(2)}) async-start(bf16[16,64,128]{2,1,0:T(8,128)(2,1)} %shard_map.128), calls=%async_computation | async-start | bytes 524288 | tf_op jit(solution)/shard_map/all_to_all | solution.py:25
  12.4 1.6 %copy-start = (bf16[2048,512]{1,0:T(8,128)(2,1)S(1)}, bf16[2048,512]{1,0:T(8,128)(2,1)}, u32[]{:S(2)}) copy-start(bf16[2048,512]{1,0:T(8,128)(2,1)} %taps.1) | copy-start | bytes 6291460
  14.0 1.0 %copy-start.5 = (bf16[560,256]{1,0:T(8,128)(2,1)S(1)}, bf16[560,256]{1,0:T(8,128)(2,1)}, u32[]{:S(2)}) copy-start(bf16[560,256]{1,0:T(8,128)(2,1)} %constant.44.clone.table) | copy-start | bytes 860164
  16.2 29.7 %copy-start.1 = (bf16[128,512]{1,0:T(8,128)(2,1)S(1)}, bf16[128,512]{1,0:T(8,128)(2,1)}, u32[]{:S(2)}) copy-start(bf16[128,512]{1,0:T(8,128)(2,1)} %out_gate.3) | copy-start | bytes 393220
  16.2 29.7 %copy-start.2 = (bf16[128,512]{1,0:T(8,128)(2,1)S(1)}, bf16[128,512]{1,0:T(8,128)(2,1)}, u32[]{:S(2)}) copy-start(bf16[128,512]{1,0:T(8,128)(2,1)} %in_gate.3) | copy-start | bytes 393220
  16.2 29.7 %copy-start.3 = (bf16[128,512]{1,0:T(8,128)(2,1)S(1)}, bf16[128,512]{1,0:T(8,128)(2,1)}, u32[]{:S(2)}) copy-start(bf16[128,512]{1,0:T(8,128)(2,1)} %values.3) | copy-start | bytes 393220
  16.2 29.7 %copy-start.4 = (bf16[128,512]{1,0:T(8,128)(2,1)S(1)}, bf16[128,512]{1,0:T(8,128)(2,1)}, u32[]{:S(2)}) copy-start(bf16[128,512]{1,0:T(8,128)(2,1)} %upstream.3) | copy-start | bytes 393220

commit v8 on v6

--- a/solution.py
+++ b/solution.py
@@ -11,7 +11,7 @@
 
 VMEM = 48 * 1024 * 1024
 PARTS = 2
-IN_FIRST, CTX_FIRST, CH_FIRST = 15, 11, 9
+IN_FIRST, CTX_FIRST, CH_FIRST = 15, 11, 11
 f32, bf16 = jnp.float32, jnp.bfloat16
 
 

time: 47.3 us -> 47.2 us (level)
  no operation moved by 1% of the time
where the time goes in v8:
time: 47.2 us; the launch traced here: 46.8 us
  blocking collectives  26.5 us (56%)
  starting transfers between devices  9.67 us (20%)
  Pallas kernels  6.13 us (13%)
  local copies, waits for them, and re-layouts  3.3 us (7%)
  between operations  0.74 us (2%)
    all_to_all x2, blocking collectives, exchange(): return lax.all_to_all(x, axis, 0, 0, tiled=True, axis_index_groups=devices)  26.5 us
    all_to_all x1, starting transfers between devices, exchange(): return lax.all_to_all(x, axis, 0, 0, tiled=True, axis_index_groups=devices)  9.67 us
    pallas_call x5, Pallas kernels, call(): pl.pallas_call(kernel, out_shape=outs, compiler_params=pltpu.CompilerPara...  6.13 us
    unnamed x20, local copies, waits for them, and re-layouts  3.3 us
  transfers between devices with their start and end apart: 1, of which 1 were waited for; matrix products, arithmetic and copies ran while one was open for 0% of the time, Pallas kernels for 3%

profile of v8, /device:TPU:1, one launch (start us, length us, event | category | flops | bytes accessed | tf_op | source)
XLA Modules:
  0.0 46.8 jit_solution(3283695381437693143)
XLA Ops:
  0.6 2.0 %shard_map.119 = bf16[16,64,128]{2,1,0:T(8,128)(2,1)} custom-call(bf16[128,512]{1,0:T(8,128)(2,1)} %out_gate.3, bf16[128,512]{1,0:T(8,128)(2,1)} %in_gate.3, bf16[128,512]{1,0:T(8,128)(2,1)} %values.3, bf16[128,512]{1,0:T(8,128)(2,1)} %upstream.3), custom_call_target="tpu_custom_call" | custom-call | flops 1000000 | bytes 1048576 | tf_op jit(solution)/shard_map/pallas_call | solution.py:211
  2.6 0.0 copy-start.2
  2.6 0.0 copy-start.7
  2.6 0.0 copy-start.9
  2.6 9.7 %all-to-all-start = ((bf16[16,64,128]{2,1,0:T(8,128)(2,1)}), bf16[16,64,128]{2,1,0:T(8,128)(2,1)S(1)}, u32[]{:S(2)}, u32[]{:S(2)}) async-start(bf16[16,64,128]{2,1,0:T(8,128)(2,1)} %shard_map.119), calls=%async_computation | async-start | bytes 524288 | tf_op jit(solution)/shard_map/all_to_all | solution.py:25
  12.3 0.1 pad_add_fusion.index
  12.4 1.6 %copy-done = bf16[2048,512]{1,0:T(8,128)(2,1)S(1)} copy-done((bf16[2048,512]{1,0:T(8,128)(2,1)S(1)}, bf16[2048,512]{1,0:T(8,128)(2,1)}, u32[]{:S(2)}) %copy-start) | copy-done | bytes 2097176
  14.0 0.9 %copy-done.1 = bf16[2,256,256]{2,1,0:T(8,128)(2,1)S(1)} copy-done((bf16[2,256,256]{2,1,0:T(8,128)(2,1)S(1)}, bf16[2,256,256]{2,1,0:T(8,128)(2,1)}, u32[]{:S(2)}) %copy-start.1) | copy-done | bytes 262168
  14.9 0.7 %copy-done.8 = f32[32,128]{1,0:T(8,128)S(1)} copy-done((f32[32,128]{1,0:T(8,128)S(1)}, f32[32,128]{1,0:T(8,128)}, u32[]{:S(2)}) %copy-start.8) | copy-done | bytes 16408
  15.6 1.3 %shard_map.120.taps_values = f32[512,256]{1,0:T(8,128)S(1)} custom-call(s32[2]{0:T(128)S(1)} %pad_add_fusion.index, bf16[2048,512]{1,0:T(8,128)(2,1)S(1)} %copy-done, f32[32,128]{1,0:T(8,128)S(1)} %copy-done.8, bf16[2,256,256]{2,1,0:T(8,128)(2,1)S(1)} %copy-done.1), custom_call_target="tpu_custom_call" | custom-call | flops 1000000 | bytes 1048576 | tf_op jit(solution)/shard_map/pallas_call | solution.py:211
  16.9 0.0 copy-start.3
  16.9 0.0 copy-start.4
  16.9 0.0 copy-start.5
  16.9 0.0 copy-start.6
  17.0 0.3 all-to-all-done.received
  17.3 0.0 copy-done.2
  17.3 0.0 copy-done.7
  17.3 0.0 copy-done.9
  17.3 1.8 %shard_map.121 = bf16[16,96,128]{2,1,0:T(8,128)(2,1)S(1)} custom-call(bf16[16,64,128]{2,1,0:T(8,128)(2,1)S(1)} %all-to-all-done.received, f32[512,256]{1,0:T(8,128)S(1)} %shard_map.120.taps_values, f32[32,128]{1,0:T(8,128)S(1)} %copy-done.9, bf16[2,256,256]{2,1,0:T(8,128)(2,1)S(1)} %copy-done.2, bf16[2,256,256]{2,1,0:T(8,128)(2,1)S(1)} %copy-done.7), custom_call_target="tpu_custom_call" | custom-call | flops 1000000 | bytes 1048576 | tf_op jit(solution)/shard_map/pallas_call | solution.py:211
  19.1 12.8 %all_to_all.15.back = bf16[16,96,128]{2,1,0:T(8,128)(2,1)S(1)} all-to-all(bf16[16,96,128]{2,1,0:T(8,128)(2,1)S(1)} %shard_map.121), channel_id=1, replica_groups={{176,192,208,224,240,0,16,32,48,64,80,96,112,128,144,160},{177,193,209,..., dimensions={0} | all-to-all | bytes 786432 | tf_op jit(solution)/shard_map/all_to_all | solution.py:25
  31.9 0.1 shard_map.122
  32.0 13.8 %all_to_all.16.arrived = bf16[16,8,512]{2,1,0:T(8,128)(2,1)S(1)} all-to-all(bf16[16,8,512]{2,1,0:T(8,128)(2,1)S(1)} %shard_map.122), channel_id=1, replica_groups={{11,12,13,14,15,0,1,2,3,4,5,6,7,8,9,10},{27,28,29,30,31,16,17,18,19,20,..., dimensions={0} | all-to-all | bytes 262144 | tf_op jit(solution)/shard_map/all_to_all | solution.py:25
  45.7 0.0 copy-done.5
  45.8 1.0 %shard_map.123 = (bf16[128,512]{1,0:T(8,128)(2,1)}, bf16[128,512]{1,0:T(8,128)(2,1)}, bf16[128,512]{1,0:T(8,128)(2,1)}, bf16[128,512]{1,0:T(8,128)(2,1)}, f32[8,8192]{1,0:T(8,128)}) custom-call(bf16[16,8,512]{2,1,0:T(8,128)(2,1)S(1)} %all_to_all.16.arrived, bf16[16,96,128]{2,1,0:T(8,128)(2,1)S(1)} %all_to_all.15.back, bf16[128,512]{1,0:T(8,128)(2,1)S(1)} %copy-done.3, ...), custom_call_target="tpu_custom_call" | custom-call | flops 1000000 | bytes 1048576 | tf_op jit(solution)/shard_map/pallas_call | solution.py:211
  (6 shorter events, 0.0 us)
Async XLA Ops:
  2.6 14.7 %copy-start.2 = (bf16[2,256,256]{2,1,0:T(8,128)(2,1)S(1)}, bf16[2,256,256]{2,1,0:T(8,128)(2,1)}, u32[]{:S(2)}) copy-start(bf16[2,256,256]{2,1,0:T(8,128)(2,1)} %constant.40.clone.matrix.forward) | copy-start | bytes 786436
  2.6 14.7 %copy-start.7 = (bf16[2,256,256]{2,1,0:T(8,128)(2,1)S(1)}, bf16[2,256,256]{2,1,0:T(8,128)(2,1)}, u32[]{:S(2)}) copy-start(bf16[2,256,256]{2,1,0:T(8,128)(2,1)} %constant.41.clone.backward) | copy-start | bytes 786436
  2.6 14.7 %copy-start.9 = (f32[32,128]{1,0:T(8,128)S(1)}, f32[32,128]{1,0:T(8,128)}, u32[]{:S(2)}) copy-start(f32[32,128]{1,0:T(8,128)} %constant.39.clone.twist) | copy-start | bytes 49156
  2.6 14.6 %all-to-all-start = ((bf16[16,64,128]{2,1,0:T(8,128)(2,1)}), bf16[16,64,128]{2,1,0:T(8,128)(2,1)S(1)}, u32[]{:S(2)}, u32[]{:S(2)}) async-start(bf16[16,64,128]{2,1,0:T(8,128)(2,1)} %shard_map.119), calls=%async_computation | async-start | bytes 524288 | tf_op jit(solution)/shard_map/all_to_all | solution.py:25
  12.4 1.6 %copy-start = (bf16[2048,512]{1,0:T(8,128)(2,1)S(1)}, bf16[2048,512]{1,0:T(8,128)(2,1)}, u32[]{:S(2)}) copy-start(bf16[2048,512]{1,0:T(8,128)(2,1)} %taps.1) | copy-start | bytes 6291460
  14.0 0.9 %copy-start.1 = (bf16[2,256,256]{2,1,0:T(8,128)(2,1)S(1)}, bf16[2,256,256]{2,1,0:T(8,128)(2,1)}, u32[]{:S(2)}) copy-start(bf16[2,256,256]{2,1,0:T(8,128)(2,1)} %constant.40.clone.matrix.forward) | copy-start | bytes 786436
  14.9 0.7 %copy-start.8 = (f32[32,128]{1,0:T(8,128)S(1)}, f32[32,128]{1,0:T(8,128)}, u32[]{:S(2)}) copy-start(f32[32,128]{1,0:T(8,128)} %constant.39.clone.twist) | copy-start | bytes 49156
  16.9 28.8 %copy-start.3 = (bf16[128,512]{1,0:T(8,128)(2,1)S(1)}, bf16[128,512]{1,0:T(8,128)(2,1)}, u32[]{:S(2)}) copy-start(bf16[128,512]{1,0:T(8,128)(2,1)} %out_gate.3) | copy-start | bytes 393220
  16.9 28.8 %copy-start.4 = (bf16[128,512]{1,0:T(8,128)(2,1)S(1)}, bf16[128,512]{1,0:T(8,128)(2,1)}, u32[]{:S(2)}) copy-start(bf16[128,512]{1,0:T(8,128)(2,1)} %in_gate.3) | copy-start | bytes 393220
  16.9 28.8 %copy-start.5 = (bf16[128,512]{1,0:T(8,128)(2,1)S(1)}, bf16[128,512]{1,0:T(8,128)(2,1)}, u32[]{:S(2)}) copy-start(bf16[128,512]{1,0:T(8,128)(2,1)} %values.3) | copy-start | bytes 393220
  16.9 28.8 %copy-start.6 = (bf16[128,512]{1,0:T(8,128)(2,1)S(1)}, bf16[128,512]{1,0:T(8,128)(2,1)}, u32[]{:S(2)}) copy-start(bf16[128,512]{1,0:T(8,128)(2,1)} %upstream.3) | copy-start | bytes 393220
